TPU v7x, 32 devices: a whole 2x2x4 slice. The times are simulated.
32 devices in a mesh: tile: 8 (over y, x, core), view: 4 (over z).
Axes of the slice: x: 2, y: 2, z: 4, core: 2. Of those that a mesh axis runs over, the one named last changes fastest.
Arguments:
- estimate: float32 [2, 112, 224, 128], P(None, 'view', 'tile'), may hold values from 0.25 to 4
- view_data: bfloat16 [4, 8, 3, 2, 58, 58, 128], P('view', 'tile'), may hold values from 0.25 to 4
- psf: float32 [6, 3, 31], replicated, may hold values from 0 to 0.5, as said below
- background: float32 [6], replicated, may hold values from 0.1 to 1
- slot_brick: int32 [4, 8, 3], P('view', 'tile'), may hold values from 0 to 7, as said below
- slot_view: int32 [4, 8, 3], P('view', 'tile'), may hold values from 0 to 5, as said below
- intersection: int32 [4, 8, 6], P('view', 'tile'), may hold values from 0 to 1, as said below
Outputs:
- updated: float32 [2, 112, 224, 128], P(None, 'view', 'tile')
Inputs may be any that keep to these rules, and one draw needn't show every extreme that they name: `slot_brick`: within a group, the jobs are exactly the pairs (brick, view) that intersection marks, each once; every brick has at least one view and one brick of each group has all 6; the jobs of a group fill its workers' 3 slots exactly. `slot_view`: the view of each job, consistent with intersection. `intersection`: each brick's row has between 1 and 6 ones. `psf`: all taps are positive.
All inputs are finite; a program needn't handle non-finite values.
Results may differ from a plain program's by a relative error of at most 0.0003.
Values may be sent and summed in bfloat16 or wider, within the bound.
A program may use at most 128 MiB of HBM per device.

v0:
```python
import jax
import jax.numpy as jnp
from jax import lax
from jax.sharding import PartitionSpec as P


def extended(array, sides, width):
    for axis, dim in sides:
        count, length = (lax.axis_size(axis), array.shape[dim])
        up = [(i, (i + 1) % count) for i in range(count - 1)]
        down = [(j, i) for i, j in up]
        last = lax.slice_in_dim(array, length - width, length, axis=dim)
        leading = lax.slice_in_dim(array, 0, width, axis=dim)
        before = lax.ppermute(last, axis, up)
        after = lax.ppermute(leading, axis, down)
        array = jnp.concatenate([before, array, after], axis=dim)
    return array


def banded(kernel_taps, order, rim_width):
    offsets = jnp.arange(order)[None, :] - jnp.arange(order)[:, None] + rim_width
    matches = offsets[:, :, None] == jnp.arange(kernel_taps.shape[0])[None, None, :]
    return jnp.sum(jnp.where(matches, kernel_taps[None, None, :], 0.0), axis=2)


def forward_blur(block, kernels, rim_width):
    band_x = banded(kernels[0], block.shape[1], rim_width)
    band_y = banded(kernels[1], block.shape[2], rim_width)
    band_z = banded(kernels[2], block.shape[3], rim_width)
    result = jnp.einsum("cxyz,wz->cxyw", block, band_z, precision=lax.Precision.HIGHEST)
    result = jnp.einsum("cxyz,vy->cxvz", result, band_y, precision=lax.Precision.HIGHEST)
    return jnp.einsum("cxyz,ux->cuyz", result, band_x, precision=lax.Precision.HIGHEST)


def backward_blur(ratio, kernels, rim_width, brick_x, brick_y):
    band_x = banded(kernels[0], ratio.shape[1], rim_width)[:, rim_width : rim_width + brick_x]
    band_y = banded(kernels[1], ratio.shape[2], rim_width)[:, rim_width : rim_width + brick_y]
    band_z = banded(kernels[2], ratio.shape[3], rim_width)
    result = jnp.einsum("cxyz,xu->cuyz", ratio, band_x, precision=lax.Precision.HIGHEST)
    result = jnp.einsum("cxyz,yv->cxvz", result, band_y, precision=lax.Precision.HIGHEST)
    return jnp.einsum("cxyz,zw->cxyw", result, band_z, precision=lax.Precision.HIGHEST)


def correction(block, measured, psf, background, view_index, rim_width, brick_x, brick_y):
    kernels = lax.dynamic_index_in_dim(psf, view_index, 0, keepdims=False)
    backdrop = lax.dynamic_index_in_dim(background, view_index, 0, keepdims=False)
    predicted = forward_blur(block, kernels, rim_width) + backdrop
    ratio = measured.astype(jnp.float32) / predicted
    return backward_blur(ratio, kernels, rim_width, brick_x, brick_y)


def on_device(estimate, view_data, psf, background, slot_brick, slot_view, intersection):
    rim_width = psf.shape[2] // 2
    channels, brick_x, brick_y, depth_cells = estimate.shape
    est_wire = estimate.astype(jnp.bfloat16)
    padded = extended(est_wire, (("tile", 2), ("view", 1)), rim_width)
    gathered = lax.all_gather(padded[None], "tile", axis=0, tiled=True)
    owners = lax.axis_size("tile")
    contrib = jnp.zeros((owners, channels, brick_x, brick_y, depth_cells), jnp.float32)
    for slot_index in range(slot_brick.shape[2]):
        brick_index = slot_brick[0, 0, slot_index]
        view_index = slot_view[0, 0, slot_index]
        block = lax.dynamic_index_in_dim(gathered, brick_index, 0, keepdims=False).astype(
            jnp.float32
        )
        factor = correction(
            block,
            view_data[0, 0, slot_index],
            psf,
            background,
            view_index,
            rim_width,
            brick_x,
            brick_y,
        )
        owner_marks = (jnp.arange(owners) == brick_index).astype(jnp.float32)
        contrib = contrib + owner_marks[:, None, None, None, None] * factor[None]
    summed = lax.psum_scatter(contrib, "tile", scatter_dimension=0, tiled=True)[0]
    views_seen = jnp.sum(intersection[0, 0]).astype(jnp.float32)
    return estimate * summed / views_seen


def solution(mesh):
    placed = (
        P(None, "view", "tile", None),
        P("view", "tile", None, None, None, None, None),
        P(),
        P(),
        P("view", "tile", None),
        P("view", "tile", None),
        P("view", "tile", None),
    )
    return jax.shard_map(
        on_device,
        mesh=mesh,
        in_specs=placed,
        out_specs=P(None, "view", "tile", None),
        check_vma=False,
    )
```

profile of v0, /device:TPU:0, one launch (start us, length us, event | category | flops | bytes accessed | tf_op | source)
XLA Modules:
  0.0 305.1 jit_solution(14112045496683728675)
XLA Ops:
  6.5 1.2 copy.95
  7.9 2.4 collective-permute-start
  10.3 1.3 collective-permute-start.1
  11.6 4.2 %collective-permute-done.1 = bf16[2,28,15,128]{3,2,1,0:T(8,128)(2,1)S(1)} collective-permute-done((bf16[2,28,15,128]{3,2,1,0:T(8,128)(2,1)S(1)}, bf16[2,28,15,128]{3,2,1,0:T(8,128)(2,1)S(1)}, u32[]{:S(2)}, u32[]{:S(2)}) %collective-permute-start.1) | collective-permute-done | bytes 215072 | tf_op jit(solution)/shard_map/ppermute | solution.py:15
  16.2 3.5 %collective-permute-start.2 = (bf16[2,15,58,128]{3,2,1,0:T(8,128)(2,1)S(1)}, bf16[2,15,58,128]{3,2,1,0:T(8,128)(2,1)S(1)}, u32[]{:S(2)}, u32[]{:S(2)}) collective-permute-start(bf16[2,15,58,128]{3,2,1,0:T(8,128)(2,1)S(1)} %get-tuple-element.17), channel_id=1, source_target_pairs={{0,1},{1,2},{2,3},{4,5},{5,6},{6,7},{8,9},{9,10},{10,11},{12,13},{... | collective-permute-start | bytes 1336328 | tf_op jit(solution)/shard_map/ppermute | solution.py:14
  19.8 1.3 collective-permute-start.3
  21.1 6.7 %collective-permute-done.2 = bf16[2,15,58,128]{3,2,1,0:T(8,128)(2,1)S(1)} collective-permute-done((bf16[2,15,58,128]{3,2,1,0:T(8,128)(2,1)S(1)}, bf16[2,15,58,128]{3,2,1,0:T(8,128)(2,1)S(1)}, u32[]{:S(2)}, u32[]{:S(2)}) %collective-permute-start.2) | collective-permute-done | bytes 445472 | tf_op jit(solution)/shard_map/ppermute | solution.py:14
  27.8 4.7 %collective-permute-done.3 = bf16[2,15,58,128]{3,2,1,0:T(8,128)(2,1)S(1)} collective-permute-done((bf16[2,15,58,128]{3,2,1,0:T(8,128)(2,1)S(1)}, bf16[2,15,58,128]{3,2,1,0:T(8,128)(2,1)S(1)}, u32[]{:S(2)}, u32[]{:S(2)}) %collective-permute-start.3) | collective-permute-done | bytes 445472 | tf_op jit(solution)/shard_map/ppermute | solution.py:15
  32.5 1.7 pad_maximum_fusion
  48.3 1.3 compare_convert_fusion
  49.6 1.4 select_reduce_fusion.7
  51.6 7.2 %fusion.59 = (bf16[1,1,1,2,58,58,128]{6,3,5,4,2,1,0:T(2,128)(2,1)}, bf16[1,1,1,2,58,58,128]{6,3,5,4,2,1,0:T(2,128)(2,1)S(1)}, bf16[1,1,1,2,58,58,128]{6,3,5,4,2,1,0:T(2,128)(2,1)}) fusion(bf16[1,1,3,2,58,58,128]{6,3,5,4,2,1,0:T(2,128)(2,1)} %param.8), kind=kLoop, calls=%fused_computation.101 | loop fusion | bytes 10334208 | tf_op jit(solution)/shard_map/slice | solution.py:68
  58.8 64.6 %all-gather.3.cloned.1.call-done = bf16[16,58,58,128]{3,2,1,0:T(8,128)(2,1)} async-done(((bf16[2,58,58,128]{3,2,1,0:T(8,128)(2,1)}), bf16[16,58,58,128]{3,2,1,0:T(8,128)(2,1)}) %all-gather.3.cloned.1.call-update) | async-done | bytes 13778960 | tf_op jit(solution)/shard_map/all_gather | solution.py:57
  123.4 3.2 %fusion.9 = f32[2,58,58,128]{3,2,1,0:T(8,128)S(1)} fusion(bf16[8,2,58,58,128]{4,3,2,1,0:T(8,128)(2,1)} %bitcast.194, s32[]{:T(128)S(6)} %select_n.75, f32[128,128]{1,0:T(8,128)S(1)} %get-tuple-element.6), kind=kOutput, calls=%fused_computation.24 | convolution fusion | flops 1322778624 | bytes 5410820 | tf_op jit(solution)/shard_map/cxyz,wz->cxyw/dot_general | solution.py:30
  126.6 3.7 %convolution_bitcast_fusion = f32[2,58,58,128]{3,2,1,0:T(8,128)S(1)} fusion(f32[2,58,58,128]{3,2,1,0:T(8,128)S(1)} %fusion.9, f32[58,58]{1,0:T(8,128)S(1)} %get-tuple-element.10), kind=kOutput, calls=%fused_computation.13 | convolution fusion | flops 599384064 | bytes 6902928 | tf_op jit(solution)/shard_map/cxyz,vy->cxvz/dot_general | solution.py:31
  130.3 5.5 %fusion = f32[58,2,58,128]{3,0,2,1:T(8,128)S(1)} fusion(f32[2,58,58,128]{3,2,1,0:T(8,128)S(1)} %convolution_bitcast_fusion, f32[58,58]{1,0:T(8,128)S(1)} %get-tuple-element.9), kind=kOutput, calls=%fused_computation.4 | convolution fusion | flops 599384064 | bytes 6902928 | tf_op jit(solution)/shard_map/cxyz,ux->cuyz/dot_general | solution.py:32
  135.8 3.5 %fusion.27 = f32[2,28,58,128]{3,1,2,0:T(8,128)S(1)} fusion(f32[58,2,58,128]{3,0,2,1:T(8,128)S(1)} %fusion, bf16[1,1,1,2,58,58,128]{6,3,5,4,2,1,0:T(2,128)(2,1)S(1)} %copy-done.2, f32[]{:T(128)} %bitcast.63, f32[58,58]{1,0:T(8,128)S(1)} %get-tuple-element.9), kind=kOutput, calls=%fused_computation.42 | convolution fusion | flops 291941376 | bytes 6843540 | tf_op jit(solution)/shard_map/cxyz,xu->cuyz/dot_general | solution.py:39
  139.3 2.0 fusion.36
  142.8 3.2 %fusion.13 = f32[2,58,58,128]{3,2,1,0:T(8,128)S(1)} fusion(bf16[8,2,58,58,128]{4,3,2,1,0:T(8,128)(2,1)} %bitcast.195, s32[]{:T(128)S(6)} %select_n.65, f32[128,128]{1,0:T(8,128)S(1)} %get-tuple-element.5), kind=kOutput, calls=%fused_computation.28 | convolution fusion | flops 1322778624 | bytes 5410820 | tf_op jit(solution)/shard_map/cxyz,wz->cxyw/dot_general | solution.py:30
  146.1 3.6 %convolution_bitcast_fusion.2 = f32[2,58,58,128]{3,2,1,0:T(8,128)S(1)} fusion(f32[2,58,58,128]{3,2,1,0:T(8,128)S(1)} %fusion.13, f32[58,58]{1,0:T(8,128)S(1)} %get-tuple-element.13), kind=kOutput, calls=%fused_computation.15 | convolution fusion | flops 599384064 | bytes 6902928 | tf_op jit(solution)/shard_map/cxyz,vy->cxvz/dot_general | solution.py:31
  149.7 5.7 %fusion.4 = f32[58,2,58,128]{3,0,2,1:T(8,128)S(1)} fusion(f32[2,58,58,128]{3,2,1,0:T(8,128)S(1)} %convolution_bitcast_fusion.2, f32[58,58]{1,0:T(8,128)S(1)} %get-tuple-element.8), kind=kOutput, calls=%fused_computation.8 | convolution fusion | flops 599384064 | bytes 6902928 | tf_op jit(solution)/shard_map/cxyz,ux->cuyz/dot_general | solution.py:32
  155.4 3.3 %fusion.29 = f32[2,28,58,128]{3,1,2,0:T(8,128)S(1)} fusion(f32[58,2,58,128]{3,0,2,1:T(8,128)S(1)} %fusion.4, bf16[1,1,1,2,58,58,128]{6,3,5,4,2,1,0:T(2,128)(2,1)S(1)} %copy-done.1, f32[]{:T(128)} %bitcast.19, f32[58,58]{1,0:T(8,128)S(1)} %get-tuple-element.8), kind=kOutput, calls=%fused_computation.44 | convolution fusion | flops 291941376 | bytes 6843540 | tf_op jit(solution)/shard_map/cxyz,xu->cuyz/dot_general | solution.py:39
  158.8 2.0 fusion.30
  160.8 3.2 %fusion.11 = f32[2,58,58,128]{3,2,1,0:T(8,128)S(1)} fusion(bf16[8,2,58,58,128]{4,3,2,1,0:T(8,128)(2,1)} %bitcast.196, s32[]{:T(128)S(6)} %select_n.70, f32[128,128]{1,0:T(8,128)S(1)} %get-tuple-element.7), kind=kOutput, calls=%fused_computation.26 | convolution fusion | flops 1322778624 | bytes 5410820 | tf_op jit(solution)/shard_map/cxyz,wz->cxyw/dot_general | solution.py:30
  164.1 4.0 %convolution_bitcast_fusion.1 = f32[2,58,58,128]{3,2,1,0:T(8,128)S(1)} fusion(f32[2,58,58,128]{3,2,1,0:T(8,128)S(1)} %fusion.11, f32[58,58]{1,0:T(8,128)S(1)} %get-tuple-element.12), kind=kOutput, calls=%fused_computation.14 | convolution fusion | flops 599384064 | bytes 6902928 | tf_op jit(solution)/shard_map/cxyz,vy->cxvz/dot_general | solution.py:31
  168.1 5.5 %fusion.2 = f32[58,2,58,128]{3,0,2,1:T(8,128)S(1)} fusion(f32[2,58,58,128]{3,2,1,0:T(8,128)S(1)} %convolution_bitcast_fusion.1, f32[58,58]{1,0:T(8,128)S(1)} %get-tuple-element.11), kind=kOutput, calls=%fused_computation.6 | convolution fusion | flops 599384064 | bytes 6902928 | tf_op jit(solution)/shard_map/cxyz,ux->cuyz/dot_general | solution.py:32
  173.6 3.4 %fusion.28 = f32[2,28,58,128]{3,1,2,0:T(8,128)S(1)} fusion(f32[58,2,58,128]{3,0,2,1:T(8,128)S(1)} %fusion.2, bf16[1,1,1,2,58,58,128]{6,3,5,4,2,1,0:T(2,128)(2,1)S(1)} %get-tuple-element.15, f32[]{:T(128)} %bitcast.41, f32[58,58]{1,0:T(8,128)S(1)} %get-tuple-element.11), kind=kOutput, calls=%fused_computation.43 | convolution fusion | flops 291941376 | bytes 6843540 | tf_op jit(solution)/shard_map/cxyz,xu->cuyz/dot_general | solution.py:39
  176.9 2.0 fusion.33
  180.5 1.1 fusion.47
  182.2 6.9 %multiply_add_fusion = f32[8,2,28,28,128]{4,1,3,2,0:T(2,128)} fusion(f32[2,28,28,128]{3,0,2,1:T(2,128)S(1)} %copy.33, f32[2,28,28,128]{3,0,2,1:T(2,128)S(1)} %copy.27, f32[2,28,28,128]{3,0,2,1:T(2,128)S(1)} %copy.21, f32[8]{0:T(128)S(1)} %get-tuple-element.45, f32[8]{0:T(128)S(1)} %get-tuple-element.46, f32[8]{0:T(128)S(1)} %compare_convert_fusion.2), kind=kLoop, calls=%fused_computation | loop fusion | flops 8028160 | bytes 8831072 | tf_op jit(solution)/shard_map/add | solution.py:77
  191.7 103.2 %all-reduce.3.cloned.1.call-done = f32[8,2,28,28,128]{4,1,3,2,0:T(2,128)} async-done(((f32[8,2,28,28,128]{4,1,3,2,0:T(2,128)}), f32[8,2,28,28,128]{4,1,3,2,0:T(2,128)}) %all-reduce.3.cloned.1.call-update) | async-done | bytes 6422544
  294.9 3.1 %fusion.40 = f32[2,28,28,128]{3,0,2,1:T(2,128)} fusion(f32[2,28,28,128]{3,0,2,1:T(2,128)S(1)} %copy-done, f32[8,2,28,28,128]{4,1,3,2,0:T(2,128)} %all-reduce.3.cloned.1.call-done, u32[]{:T(128)} %bitcast.86, f32[]{:T(128)S(6)} %convert_element_type.58), kind=kLoop, calls=%fused_computation.59 | loop fusion | flops 401408 | bytes 2408456 | tf_op jit(solution)/shard_map/div | solution.py:80
  (43 shorter events, 9.5 us)
Async XLA Ops:
  6.5 116.8 %all-gather.3.cloned.1.call-start = ((), (), s32[]{:S(2)}) async-start(), calls=%async_computation | async-start | bytes 17104896 | tf_op jit(solution)/shard_map/all_gather | solution.py:57
  7.9 3.7 %collective-permute-start = (bf16[2,28,15,128]{3,2,1,0:T(8,128)(2,1)S(1)}, bf16[2,28,15,128]{3,2,1,0:T(8,128)(2,1)S(1)}, u32[]{:S(2)}, u32[]{:S(2)}) collective-permute-start(bf16[2,28,15,128]{3,2,1,0:T(8,128)(2,1)S(1)} %get-tuple-element.19), channel_id=1, source_target_pairs={{0,4},{4,8},{8,12},{12,16},{16,20},{20,24},{24,28},{1,5},{5,9},{9,... | collective-permute-start | bytes 645128 | tf_op jit(solution)/shard_map/ppermute | solution.py:14
  10.3 5.5 %collective-permute-start.1 = (bf16[2,28,15,128]{3,2,1,0:T(8,128)(2,1)S(1)}, bf16[2,28,15,128]{3,2,1,0:T(8,128)(2,1)S(1)}, u32[]{:S(2)}, u32[]{:S(2)}) collective-permute-start(bf16[2,28,15,128]{3,2,1,0:T(8,128)(2,1)S(1)} %get-tuple-element.20), channel_id=1, source_target_pairs={{4,0},{8,4},{12,8},{16,12},{20,16},{24,20},{28,24},{5,1},{9,5},{13... | collective-permute-start | bytes 645128 | tf_op jit(solution)/shard_map/ppermute | solution.py:15
  16.1 18.2 %copy-start.3 = (s32[1,1,3]{2,1,0:T(1,128)S(1)}, s32[1,1,3]{2,1,0:T(1,128)}, u32[]{:S(2)}) copy-start(s32[1,1,3]{2,1,0:T(1,128)} %param.11) | copy-start | bytes 40
  16.1 22.7 %copy-start.4 = (s32[1,1,3]{2,1,0:T(1,128)S(1)}, s32[1,1,3]{2,1,0:T(1,128)}, u32[]{:S(2)}) copy-start(s32[1,1,3]{2,1,0:T(1,128)} %param.12) | copy-start | bytes 40
  16.1 30.8 %copy-start.5 = (f32[6]{0:T(128)S(1)}, f32[6]{0:T(128)}, u32[]{:S(2)}) copy-start(f32[6]{0:T(128)} %param.10) | copy-start | bytes 76
  16.1 33.4 %copy-start.6 = (f32[6,3,31]{2,1,0:T(4,128)S(1)}, f32[6,3,31]{2,1,0:T(4,128)}, u32[]{:S(2)}) copy-start(f32[6,3,31]{2,1,0:T(4,128)} %param.9) | copy-start | bytes 6700
  16.2 11.5 %collective-permute-start.2 = (bf16[2,15,58,128]{3,2,1,0:T(8,128)(2,1)S(1)}, bf16[2,15,58,128]{3,2,1,0:T(8,128)(2,1)S(1)}, u32[]{:S(2)}, u32[]{:S(2)}) collective-permute-start(bf16[2,15,58,128]{3,2,1,0:T(8,128)(2,1)S(1)} %get-tuple-element.17), channel_id=1, source_target_pairs={{0,1},{1,2},{2,3},{4,5},{5,6},{6,7},{8,9},{9,10},{10,11},{12,13},{... | collective-permute-start | bytes 1336328 | tf_op jit(solution)/shard_map/ppermute | solution.py:14
  19.8 12.7 %collective-permute-start.3 = (bf16[2,15,58,128]{3,2,1,0:T(8,128)(2,1)S(1)}, bf16[2,15,58,128]{3,2,1,0:T(8,128)(2,1)S(1)}, u32[]{:S(2)}, u32[]{:S(2)}) collective-permute-start(bf16[2,15,58,128]{3,2,1,0:T(8,128)(2,1)S(1)} %get-tuple-element.18), channel_id=1, source_target_pairs={{1,0},{2,1},{3,2},{5,4},{6,5},{7,6},{9,8},{10,9},{11,10},{13,12},{... | collective-permute-start | bytes 1336328 | tf_op jit(solution)/shard_map/ppermute | solution.py:15
  34.2 260.7 %all-reduce.3.cloned.1.call-start = ((), (), s32[]{:S(2)}) async-start(), calls=%async_computation.1 | async-start | bytes 12845056
  130.3 5.5 %copy-start.2 = (bf16[1,1,1,2,58,58,128]{6,3,5,4,2,1,0:T(2,128)(2,1)S(1)}, bf16[1,1,1,2,58,58,128]{6,3,5,4,2,1,0:T(2,128)(2,1)}, u32[]{:S(2)}) copy-start(bf16[1,1,1,2,58,58,128]{6,3,5,4,2,1,0:T(2,128)(2,1)} %get-tuple-element.16) | copy-start | bytes 5167108
  149.7 5.7 %copy-start.1 = (bf16[1,1,1,2,58,58,128]{6,3,5,4,2,1,0:T(2,128)(2,1)S(1)}, bf16[1,1,1,2,58,58,128]{6,3,5,4,2,1,0:T(2,128)(2,1)}, u32[]{:S(2)}) copy-start(bf16[1,1,1,2,58,58,128]{6,3,5,4,2,1,0:T(2,128)(2,1)} %get-tuple-element.14) | copy-start | bytes 5167108
  189.1 0.7 copy-start.7
  189.1 1.9 copy-start.8
  189.1 105.8 %copy-start = (f32[2,28,28,128]{3,0,2,1:T(2,128)S(1)}, f32[2,28,28,128]{3,0,2,1:T(2,128)}, u32[]{:S(2)}) copy-start(f32[2,28,28,128]{3,0,2,1:T(2,128)} %param.7) | copy-start | bytes 2408452
Sparse Core Ops, SparseCore 0:
  34.4 88.9 all-gather.2
  189.3 105.6 all-reduce.2
where the time goes:
time: 310 us; the launch traced here: 305 us
  waiting for transfers between devices  183 us (59%)
  matrix products  56.7 us (18%)
  between operations  26 us (8%)
  other arithmetic  16.6 us (5%)
  local copies, waits for them, and re-layouts  13.8 us (4%)
  starting transfers between devices  8.51 us (3%)
    unnamed x3, waiting for transfers between devices  103 us
    all_gather x1, waiting for transfers between devices, on_device(): gathered = lax.all_gather(padded[None], 'tile', axis=0, tiled=True)  64.6 us
    dot_general x3, matrix products, forward_blur(): jnp.einsum('cxyz,ux->cuyz', result, band_x, precision=lax.Precision.HIGHEST)  16.6 us
    dot_general x3, matrix products, forward_blur(): jnp.einsum('cxyz,vy->cxvz', result, band_y, precision=lax.Precision.HIGHEST)  11.3 us
    dot_general x3, matrix products, backward_blur(): jnp.einsum('cxyz,xu->cuyz', ratio, band_x, precision=lax.Precision.HIGHEST)  10.2 us
    dot_general x3, matrix products, forward_blur(): jnp.einsum('cxyz,wz->cxyw', block, band_z, precision=lax.Precision.HIGHEST)  9.73 us
    ppermute x2, waiting for transfers between devices, extended(): after = lax.ppermute(leading, axis, down)  8.87 us
    slice x1, local copies, waits for them, and re-layouts, on_device(): view_data[0, 0, slot_index]  7.17 us
  transfers between devices with their start and end apart: 6, of which 5 were waited for; matrix products, arithmetic and copies ran while one was open for 5% of the time, Pallas kernels for 0%

commit v1 on v0

v1 whole, which is shorter than its diff:
```python
import functools

import jax
import jax.numpy as jnp
from jax import lax
from jax.experimental import pallas as pl
from jax.experimental.pallas import tpu as pltpu
from jax.sharding import PartitionSpec as P

MESH = pl.DeviceIdType.MESH
F32 = jnp.float32
BF16 = jnp.bfloat16
ROWS = 64
HB = 16
UP = 32
PITCH1 = 72
PITCH2 = 40
VMEM = pl.BlockSpec(memory_space=pltpu.VMEM)
SMEM = pl.BlockSpec(memory_space=pltpu.SMEM)


def place(n):
    t, v = lax.axis_index("tile"), lax.axis_index("view")
    sib = t + 1 - 2 * lax.rem(t, 2)
    return t, v, sib


def same(t, step, n):
    return lax.rem(t + 2 * step + 2 * n, n)


def greet(n, nv, with_view):
    t, v, sib = place(n)
    barrier = pltpu.get_barrier_semaphore()

    def signal(tile, view):
        pl.semaphore_signal(barrier, inc=1, device_id=(tile, view), device_id_type=MESH)

    signal(sib, v)
    for k in range(1, n // 2):
        signal(same(t, k, n), v)
    peers = n // 2
    if with_view:

        @pl.when(v > 0)
        def _():
            signal(t, v - 1)

        @pl.when(v < nv - 1)
        def _():
            signal(t, v + 1)

        peers = peers + jnp.minimum(v, 1) + jnp.minimum(nv - 1 - v, 1)
    pl.semaphore_wait(barrier, peers)


class Gather:
    def __init__(self, n, nv, by, halo, wire, out, sems):
        self.n, self.nv, self.by, self.halo = n, nv, by, halo
        self.wire, self.out = wire, out
        self.sm, self.rm, self.sz, self.rz, self.ss, self.rs, self.loc = sems
        self.t, self.v, self.sib = place(n)

    def slab(self, c, b, part):
        start, size = ((HB, 2 * HB), (0, HB), (3 * HB, HB))[part]
        return self.out.at[c, pl.ds(self.halo + self.by * b, self.by), pl.ds(start, size), :]

    def copy(self, src, dst, s, r, dev):
        return pltpu.make_async_remote_copy(
            src_ref=src, dst_ref=dst, send_sem=s, recv_sem=r, device_id=dev, device_id_type=MESH
        )

    def main(self, c, k):
        return self.copy(
            self.wire.at[c],
            self.slab(c, self.t, 0),
            self.sm.at[c, k],
            self.rm.at[c, k],
            (same(self.t, k, self.n), self.v),
        )

    def to_sib(self, c, k, part):
        b = same(self.t, -k, self.n)
        src = self.wire.at[c] if (k == 0 and part == 0) else self.slab(c, b, part)
        return self.copy(
            src, self.slab(c, b, part), self.ss.at[c, k, part], self.rs.at[c, k, part], (self.sib, self.v)
        )

    def to_view(self, c, k, up):
        b = same(self.t, -k, self.n)
        first = HB if up else 0
        if k == 0:
            src = self.wire.at[c, :, pl.ds(first, HB), :]
        else:
            src = self.out.at[c, pl.ds(self.halo + self.by * b, self.by), pl.ds(HB + first, HB), :]
        side = 0 if up else 1
        return self.copy(
            src,
            self.slab(c, b, 1 if up else 2),
            self.sz.at[c, k, side],
            self.rz.at[c, k, side],
            (self.t, self.v + 1 if up else self.v - 1),
        )

    def local(self, c):
        return pltpu.make_async_copy(self.wire.at[c], self.slab(c, self.t, 0), self.loc.at[c])

    def views(self, c, k, act):
        @pl.when(self.v < self.nv - 1)
        def _():
            act(self.to_view(c, k, True))

        @pl.when(self.v > 0)
        def _():
            act(self.to_view(c, k, False))

    def zeros(self):
        count = self.out.shape[1]
        last = self.halo + self.by * self.n

        def clear(where):
            self.out[where] = jnp.zeros(self.out.at[where].shape, BF16)

        def edge(i, _):
            for c in range(2):
                self.out[c, pl.ds(i, 1)] = jnp.zeros((1,) + self.out.shape[2:], BF16)
            return 0

        lax.fori_loop(0, self.halo, edge, 0)
        lax.fori_loop(last, count, edge, 0)

        def rows(start):
            def body(i, _):
                for c in range(2):
                    self.out[c, pl.ds(i, 1), pl.ds(start, HB), :] = jnp.zeros((1, HB, 128), BF16)
                return 0

            lax.fori_loop(self.halo, last, body, 0)

        @pl.when(self.v == 0)
        def _():
            rows(0)

        @pl.when(self.v == self.nv - 1)
        def _():
            rows(3 * HB)

    def begin(self, c):
        for k in range(1, self.n // 2):
            self.main(c, k).start()
        self.views(c, 0, lambda d: d.start())
        self.to_sib(c, 0, 0).start()
        self.local(c).start()

    def forward(self, c):
        for k in range(1, self.n // 2):
            self.main(c, k).wait_recv()
            self.views(c, k, lambda d: d.start())
            self.to_sib(c, k, 0).start()

        def side(k, part, when):
            @pl.when(when)
            def _():
                self.to_view(c, k, part == 1).wait_recv()
                self.to_sib(c, k, part).start()

        for k in range(self.n // 2):
            side(k, 1, self.v > 0)
            side(k, 2, self.v < self.nv - 1)

    def arrive(self, c):
        self.local(c).wait()
        for k in range(self.n // 2):
            self.to_sib(c, k, 0).wait_recv()

            @pl.when(self.v > 0)
            def _():
                self.to_sib(c, k, 1).wait_recv()

            @pl.when(self.v < self.nv - 1)
            def _():
                self.to_sib(c, k, 2).wait_recv()

    def finish(self, c):
        for k in range(self.n // 2):
            if k:
                self.main(c, k).wait_send()
            self.views(c, k, lambda d: d.wait_send())
            self.to_sib(c, k, 0).wait_send()

            @pl.when(self.v > 0)
            def _():
                self.to_sib(c, k, 1).wait_send()

            @pl.when(self.v < self.nv - 1)
            def _():
                self.to_sib(c, k, 2).wait_send()


def gather_sems(n):
    q = n // 2
    dma = pltpu.SemaphoreType.DMA
    return [dma((2, q)), dma((2, q)), dma((2, q, 2)), dma((2, q, 2)), dma((2, q, 3)), dma((2, q, 3)), dma((2,))]


def gather_kernel(n, nv, by, halo, wire, out, *sems):
    g = Gather(n, nv, by, halo, wire, out, sems)
    greet(n, nv, True)
    g.begin(0)
    g.begin(1)
    g.zeros()
    for c in range(2):
        g.forward(c)
    for c in range(2):
        g.arrive(c)
        g.finish(c)


def iota(shape, dim):
    return lax.broadcasted_iota(jnp.int32, shape, dim)


def split(x):
    hi = x.astype(BF16)
    return hi, (x - hi.astype(F32)).astype(BF16)


def band(tap, count, index, valid):
    index = jnp.where(valid, index, -1)
    total = jnp.zeros(index.shape, F32)
    for k in range(count):
        total = jnp.where(index == k, tap(k), total)
    return total


def build_bands(tap, dims, mats):
    fx, fy, cx, cy, fz, cz = mats
    taps, halo, bx, by, nz = dims
    px, py = bx + 2 * halo, by + 2 * halo

    def pieces(value, low):
        hi, lo = split(value)
        return jnp.where(low, lo.astype(F32), hi.astype(F32)).astype(BF16)

    p, col = iota((ROWS, 3 * ROWS), 0), iota((ROWS, 3 * ROWS), 1)
    low = (col >= ROWS) & (col < 2 * ROWS)
    r = jnp.where(col >= 2 * ROWS, col - 2 * ROWS, jnp.where(col >= ROWS, col - ROWS, col))
    gap = 2 * HB - (bx - HB) + HB
    x = jnp.where(r < 2 * HB, r - HB, r - gap + HB)
    fresh = (r < 2 * HB) | (x >= HB)
    q = x + halo
    valid = fresh & (q >= 0) & (q < px) & (p < px)
    fx[...] = pieces(band(lambda k: tap(0, k), taps, q - p + halo, valid), low)
    fy[...] = pieces(band(lambda k: tap(1, k), taps, r - p + halo, (r < py) & (p < py)), low)
    p, r, low = p[:UP], r[:UP], low[:UP]
    cx[...] = pieces(band(lambda k: tap(0, k), taps, p - r + 2 * halo, (r < px) & (p < bx)), low)
    cy[...] = pieces(band(lambda k: tap(1, k), taps, p - r + 2 * halo, (r < py) & (p < by)), low)
    row, w = iota((2 * nz, nz), 0), iota((2 * nz, nz), 1)
    z = jnp.where(row >= nz, row - nz, row)
    fz[...] = pieces(band(lambda k: tap(2, k), taps, z - w + halo, w < nz), row >= nz)
    back = band(lambda k: tap(2, k), taps, w - z + halo, w < nz)
    hi, lo = split(back)
    cz[...] = jnp.concatenate([hi, lo], axis=1)


def stack(a, b):
    ah, al = split(a)
    bh, bl = split(b)
    hi = jnp.concatenate([ah, bh], axis=1)
    lo = jnp.concatenate([al, bl], axis=1)
    return jnp.concatenate([hi, hi, lo], axis=0)


def dot(a, b):
    return jnp.dot(a, b, preferred_element_type=F32)


def job(block, view, backdrop, dims, mats, s1, s2, s3, emit):
    fx, fy, cx, cy, fz, cz = mats
    taps, halo, bx, by, nz = dims
    px, py = bx + 2 * halo, by + 2 * halo
    chunk = 8

    def first(i, _):
        e = block(i * chunk, chunk).reshape(chunk * ROWS, nz)
        t = dot(jnp.concatenate([e, e], axis=1), fz[...])
        for j in range(0, chunk, 2):
            a, b = t[j * ROWS : (j + 1) * ROWS], t[(j + 1) * ROWS : (j + 2) * ROWS]
            u = dot(fx[...], stack(a, b))
            y = i * chunk + j
            s1[pl.ds(pl.multiple_of(y * PITCH1, 8), ROWS), :] = u[:, :nz]
            s1[pl.ds(pl.multiple_of((y + 1) * PITCH1, 8), ROWS), :] = u[:, nz:]
        return 0

    lax.fori_loop(0, ROWS // chunk, first, 0)

    def second(i, _):
        x = 2 * i
        a = s1[pl.ds(x, ROWS, PITCH1), :]
        b = s1[pl.ds(x + 1, ROWS, PITCH1), :]
        predicted = dot(fy[...], stack(a, b)) + backdrop
        pad = jnp.zeros((ROWS - py, nz), F32)
        va = jnp.concatenate([view(x).astype(F32), pad], axis=0)
        vb = jnp.concatenate([view(x + 1).astype(F32), pad], axis=0)
        f = dot(cy[...], stack(va / predicted[:, :nz], vb / predicted[:, nz:]))
        s2[pl.ds(pl.multiple_of(x * PITCH2, 8), UP), :] = f[:, :nz]
        s2[pl.ds(pl.multiple_of((x + 1) * PITCH2, 8), UP), :] = f[:, nz:]
        return 0

    lax.fori_loop(0, px // 2, second, 0)

    def third(i, _):
        y = 2 * i
        a = s2[pl.ds(y, ROWS, PITCH2), :]
        b = s2[pl.ds(y + 1, ROWS, PITCH2), :]
        f = dot(cx[...], stack(a, b))
        s3[pl.ds(pl.multiple_of(y * UP, 8), UP), :] = f[:, :nz]
        s3[pl.ds(pl.multiple_of((y + 1) * UP, 8), UP), :] = f[:, nz:]
        return 0

    lax.fori_loop(0, by // 2, third, 0)
    piece = by * UP // 4

    def fourth(i, _):
        rows = pl.ds(pl.multiple_of(i * piece, 8), piece)
        hi, lo = split(s3[rows, :])
        out = dot(jnp.concatenate([hi, lo], axis=1), cz[...])
        emit(rows, out[:, :nz] + out[:, nz:])
        return 0

    lax.fori_loop(0, 4, fourth, 0)


def job_scratch(by, nz):
    return [
        pltpu.VMEM((ROWS, 3 * ROWS), BF16),
        pltpu.VMEM((ROWS, 3 * ROWS), BF16),
        pltpu.VMEM((UP, 3 * ROWS), BF16),
        pltpu.VMEM((UP, 3 * ROWS), BF16),
        pltpu.VMEM((2 * nz, nz), BF16),
        pltpu.VMEM((2 * nz, 2 * nz), BF16),
        pltpu.VMEM((ROWS * PITCH1, nz), F32),
        pltpu.VMEM((ROWS * PITCH2, nz), F32),
        pltpu.VMEM((by * UP, nz), F32),
    ]


def jobs_kernel(n, dims, gathered, views, psf, background, bricks, slot_views, contrib, *scratch):
    mats, (s1, s2, s3) = scratch[:6], scratch[6:]
    taps, halo, bx, by, nz = dims
    s, c = pl.program_id(0), pl.program_id(1)
    brick, view = bricks[s], slot_views[s]

    @pl.when((s == 0) & (c == 0))
    def _():
        s2[...] = jnp.zeros_like(s2)

    @pl.when(c == 0)
    def _():
        build_bands(lambda a, k: psf[(view * 3 + a) * taps + k], dims, mats)

    def block(y, count):
        return gathered[c, pl.ds(brick * by + y, count)]

    def emit(rows, value):
        @pl.when(s == 0)
        def _():
            for o in range(n):
                contrib[o, c, rows, :] = jnp.where(brick == o, value, 0.0)

        @pl.when(s > 0)
        def _():
            contrib[brick, c, rows, :] += value

    job(block, lambda x: views[0, 0, x], background[view], dims, mats, s1, s2, s3, emit)


class Scatter:
    def __init__(self, n, by, nz, contrib, rx1, code, scale, code_in, scale_in, sems):
        self.n, self.nz, self.rows = n, nz, by * UP
        self.contrib, self.rx1 = contrib, rx1
        self.code, self.scale, self.code_in, self.scale_in = code, scale, code_in, scale_in
        self.s1, self.r1, self.s2, self.r2 = sems
        self.t, self.v, self.sib = place(n)

    def pair(self, c, j):
        return pltpu.make_async_remote_copy(
            src_ref=self.contrib.at[same(self.sib, j, self.n), c],
            dst_ref=self.rx1.at[j, c],
            send_sem=self.s1.at[j, c],
            recv_sem=self.r1.at[j, c],
            device_id=(self.sib, self.v),
            device_id_type=MESH,
        )

    def chip(self, c, j, kind):
        src, dst = ((self.code, self.code_in), (self.scale, self.scale_in))[kind]
        return pltpu.make_async_remote_copy(
            src_ref=src.at[j, c],
            dst_ref=dst.at[j, c],
            send_sem=self.s2.at[j, c, kind],
            recv_sem=self.r2.at[j, c, kind],
            device_id=(same(self.t, j, self.n), self.v),
            device_id_type=MESH,
        )

    def order(self):
        return list(range(1, self.n // 2)) + [0]

    def begin(self, c):
        for j in self.order():
            self.pair(c, j).start()

    def send(self, c):
        piece = 128
        for j in range(1, self.n // 2):
            self.pair(c, j).wait_recv()
            o = same(self.t, j, self.n)

            def add(i, top):
                rows = pl.ds(pl.multiple_of(i * piece, 8), piece)
                value = self.contrib[o, c, rows, :] + self.rx1[j, c, rows, :]
                self.rx1[j, c, rows, :] = value
                return jnp.maximum(top, jnp.max(value.reshape(piece // 8, 8, self.nz), axis=0))

            top = lax.fori_loop(0, self.rows // piece, add, jnp.zeros((8, self.nz), F32))
            top = jnp.max(top, axis=0, keepdims=True)
            top = jnp.where(top > 0.0, top, 1.0)
            self.scale[j, c] = jnp.broadcast_to(top, (8, self.nz))
            gain = 1.0 / top

            def pack(i, _):
                rows = pl.ds(pl.multiple_of(i * piece, 16), piece)
                level = jnp.minimum(self.rx1[j, c, rows, :] * gain * 65535.0, 65535.0)
                whole = jnp.round(level).astype(jnp.int32) - 32768
                self.code[j, c, rows, :] = whole.astype(jnp.int16)
                return 0

            lax.fori_loop(0, self.rows // piece, pack, 0)
            self.chip(c, j, 0).start()
            self.chip(c, j, 1).start()

    def total(self, c):
        piece = 128
        q = self.n // 2
        self.pair(c, 0).wait_recv()
        for j in range(1, q):
            self.chip(c, j, 0).wait_recv()
            self.chip(c, j, 1).wait_recv()

        def add(i, _):
            rows = pl.ds(pl.multiple_of(i * piece, 16), piece)
            value = self.contrib[self.t, c, rows, :] + self.rx1[0, c, rows, :]
            for j in range(1, q):
                level = self.code_in[j, c, rows, :].astype(jnp.int32).astype(F32) + 32768.0
                value = value + level * (self.scale_in[j, c, 0:1, :] * (1.0 / 65535.0))
            self.rx1[0, c, rows, :] = value
            return 0

        lax.fori_loop(0, self.rows // piece, add, 0)

    def finish(self, c):
        for j in range(self.n // 2):
            self.pair(c, j).wait_send()
            if j:
                self.chip(c, j, 0).wait_send()
                self.chip(c, j, 1).wait_send()


def scatter_scratch(n, by, nz):
    q, rows = n // 2, by * UP
    dma = pltpu.SemaphoreType.DMA
    return [
        pltpu.VMEM((q, 2, rows, nz), F32),
        pltpu.VMEM((q, 2, rows, nz), jnp.int16),
        pltpu.VMEM((q, 2, 8, nz), F32),
        pltpu.VMEM((q, 2, rows, nz), jnp.int16),
        pltpu.VMEM((q, 2, 8, nz), F32),
        dma((q, 2)),
        dma((q, 2)),
        dma((q, 2, 2)),
        dma((q, 2, 2)),
    ]


def update(c, estimate, out, total, seen):
    bx, by = estimate.shape[1:3]

    def body(u, _):
        out[c, u] = estimate[c, u] * total[pl.ds(u, by, UP), :] / seen
        return 0

    lax.fori_loop(0, bx, body, 0)


def scatter_kernel(n, nv, contrib, estimate, seen_ref, out, rx1, code, scale, code_in, scale_in, *rest):
    by, nz = estimate.shape[2:]
    sems, final = rest[:4], rest[4]
    s = Scatter(n, by, nz, contrib, rx1, code, scale, code_in, scale_in, sems)
    greet(n, nv, False)
    s.begin(0)
    s.begin(1)
    seen = seen_ref[0]
    for c in range(2):
        s.send(c)
    for c in range(2):
        s.total(c)

        def move(i, _):
            rows = pl.ds(pl.multiple_of(i * 128, 8), 128)
            final[rows, :] = rx1[0, c, rows, :]
            return 0

        lax.fori_loop(0, by * UP // 128, move, 0)
        update(c, estimate, out, final, seen)
        s.finish(c)


def on_device(n, nv, estimate, view_data, psf, background, slot_brick, slot_view, intersection):
    channels, bx, by, nz = estimate.shape
    taps = psf.shape[2]
    halo = taps // 2
    dims = (taps, halo, bx, by, nz)
    slots, px, py = slot_brick.shape[2], bx + 2 * halo, by + 2 * halo
    est_wire = jnp.swapaxes(estimate.astype(BF16), 1, 2)
    wire = jnp.concatenate([est_wire[:, :, :HB], est_wire[:, :, bx - HB :]], axis=2)
    count = 2 * halo + by * n + ROWS - py
    limit = 56 * 1024 * 1024
    gathered = pl.pallas_call(
        functools.partial(gather_kernel, n, nv, by, halo),
        out_shape=jax.ShapeDtypeStruct((channels, count, ROWS, nz), BF16),
        in_specs=[VMEM],
        out_specs=VMEM,
        scratch_shapes=gather_sems(n),
        compiler_params=pltpu.CompilerParams(collective_id=0, has_side_effects=True, vmem_limit_bytes=limit),
    )(wire)
    whole = lambda *shape: pl.BlockSpec(shape, lambda s, c: (0,) * len(shape))
    contrib = pl.pallas_call(
        functools.partial(jobs_kernel, n, dims),
        grid=(slots, channels),
        out_shape=jax.ShapeDtypeStruct((n, channels, by * UP, nz), F32),
        in_specs=[
            whole(channels, count, ROWS, nz),
            pl.BlockSpec((1, 1, px, py, nz), lambda s, c: (s, c, 0, 0, 0)),
            SMEM,
            SMEM,
            SMEM,
            SMEM,
        ],
        out_specs=whole(n, channels, by * UP, nz),
        scratch_shapes=job_scratch(by, nz),
        compiler_params=pltpu.CompilerParams(vmem_limit_bytes=limit),
    )(gathered, view_data[0, 0], psf.reshape(-1), background, slot_brick[0, 0], slot_view[0, 0])
    seen = jnp.sum(intersection[0, 0]).astype(F32).reshape(1)
    return pl.pallas_call(
        functools.partial(scatter_kernel, n, nv),
        out_shape=jax.ShapeDtypeStruct(estimate.shape, F32),
        in_specs=[VMEM, VMEM, SMEM],
        out_specs=VMEM,
        scratch_shapes=scatter_scratch(n, by, nz) + [pltpu.VMEM((by * UP, nz), F32)],
        compiler_params=pltpu.CompilerParams(collective_id=1, has_side_effects=True, vmem_limit_bytes=limit),
    )(contrib, estimate, seen)


def solution(mesh):
    placed = (
        P(None, "view", "tile", None),
        P("view", "tile", None, None, None, None, None),
        P(),
        P(),
        P("view", "tile", None),
        P("view", "tile", None),
        P("view", "tile", None),
    )
    return jax.shard_map(
        functools.partial(on_device, mesh.shape["tile"], mesh.shape["view"]),
        mesh=mesh,
        in_specs=placed,
        out_specs=P(None, "view", "tile", None),
        check_vma=False,
    )
```

time: 310 us -> 184 us (0.59); the launches traced: 305 us -> 184 us
  waiting for transfers between devices: 183 us -> 0 us
  Pallas kernels: 0 us -> 172 us
  matrix products: 56.7 us -> 0 us
  between operations: 26 us -> 0.73 us
  other arithmetic: 16.6 us -> 3 us
  starting transfers between devices: 8.51 us -> 0 us
  local copies, waits for them, and re-layouts: 13.8 us -> 8.58 us
    pallas_call x0 -> x3, Pallas kernels: none -> 172 us  [the longest x1 102 us: on_device(): pl.pallas_call(functools.partial(jobs_kernel, n, dims), grid=(slots, chan...]
    unnamed x3 -> x0, waiting for transfers between devices: 103 us -> none
    all_gather x1 -> x0, waiting for transfers between devices: 64.6 us -> none  [on_device(): gathered = lax.all_gather(padded[None], 'tile', axis=0, tiled=True)]
    dot_general x18 -> x0, matrix products: 56.7 us -> none  [the longest x3 16.6 us: forward_blur(): jnp.einsum('cxyz,ux->cuyz', result, band_x, precision=lax.Precision.HIGHEST)]
    ppermute x4 -> x0, waiting for transfers between devices: 15.6 us -> none  [the longest x2 8.87 us: extended(): after = lax.ppermute(leading, axis, down)]
    slice x5 -> x1, local copies, waits for them, and re-layouts: 8.67 us -> 0.1 us  [on_device(): est_wire[:, :, :HB]]
    ppermute x4 -> x0, starting transfers between devices: 8.47 us -> none  [the longest x2 5.88 us: extended(): before = lax.ppermute(last, axis, up)]
    add x3 -> x0, other arithmetic: 6.91 us -> none  [the longest x1 6.89 us: on_device(): contrib = contrib + owner_marks[:, None, None, None, None] * factor[None]]
  transfers between devices with their start and end apart: 6 -> 0, of which waited for: 5 -> 0; matrix products, arithmetic and copies ran while one was open for 5% -> 0% of each run, Pallas kernels for 0% -> 0%
where the time goes in v1:
time: 184 us
  Pallas kernels  172 us (93%)
  local copies, waits for them, and re-layouts  8.58 us (5%)
  other arithmetic  3 us (2%)
    pallas_call x1, Pallas kernels, on_device(): pl.pallas_call(functools.partial(jobs_kernel, n, dims), grid=(slots, chan...  102 us
    pallas_call x1, Pallas kernels, on_device(): pl.pallas_call(functools.partial(gather_kernel, n, nv, by, halo), out_sha...  38.3 us
    pallas_call x1, Pallas kernels, on_device(): pl.pallas_call(functools.partial(scatter_kernel, n, nv), out_shape=jax.Sh...  31.6 us
    unnamed x12, local copies, waits for them, and re-layouts  5.03 us

profile of v1, /device:TPU:0, one launch (start us, length us, event | category | flops | bytes accessed | tf_op | source)
XLA Modules:
  0.0 184.2 jit_solution(13663519974989285871)
XLA Ops:
  0.0 0.0 slice-start
  0.0 1.6 convert_element_type.6
  1.6 0.1 copy.19
  1.7 0.1 fusion
  1.8 0.8 pad_maximum_fusion.wire
  2.6 0.0 slice-start.1
  2.6 38.3 %shard_map.73.gathered = bf16[2,260,64,128]{3,2,1,0:T(8,128)(2,1)} custom-call(bf16[2,28,32,128]{3,2,1,0:T(8,128)(2,1)} %pad_maximum_fusion.wire), custom_call_target="tpu_custom_call" | custom-call | tf_op jit(solution)/shard_map/pallas_call | solution.py:529
  40.8 0.0 slice-done
  40.9 0.0 slice-done.1
  40.9 0.0 copy-start.1
  40.9 3.9 %copy.18 = bf16[1,1,3,2,58,58,128]{6,5,4,3,2,1,0:T(8,128)(2,1)} copy(bf16[1,1,3,2,58,58,128]{6,3,5,4,2,1,0:T(2,128)(2,1)S(1)} %bitcast.11) | data formatting | bytes 10334208 | tf_op args[1]
  44.8 0.0 copy-done.1
  44.8 0.7 reshape.6.psf
  45.5 0.0 copy-start
  45.5 0.0 copy-start.2
  45.5 102.0 %shard_map.74.contrib = f32[8,2,896,128]{3,2,1,0:T(8,128)} custom-call(bf16[2,260,64,128]{3,2,1,0:T(8,128)(2,1)} %shard_map.73.gathered, bf16[3,2,58,58,128]{4,3,2,1,0:T(8,128)(2,1)} %bitcast.9, f32[558]{0:T(1024)} %reshape.6.psf, f32[6]{0:T(128)} %background.1, s32[3]{0:T(128)} %bitcast.13, s32[3]{0:T(128)} %bitcast.14), custom_call_target="tpu_custom_call" | custom-call | tf_op jit(solution)/shard_map/pallas_call | solution.py:538
  147.6 0.0 copy-done
  147.6 1.1 copy.14.estimate
  148.6 0.0 copy-done.2
  148.6 0.6 reduce_sum.9
  149.9 31.6 %shard_map.75 = f32[2,28,28,128]{3,2,1,0:T(8,128)} custom-call(f32[8,2,896,128]{3,2,1,0:T(8,128)} %shard_map.74.contrib, f32[2,28,28,128]{3,2,1,0:T(8,128)} %copy.14.estimate, f32[1]{0:T(128)} %bitcast.4.seen_ref), custom_call_target="tpu_custom_call" | custom-call | tf_op jit(solution)/shard_map/pallas_call | solution.py:555
  181.5 2.7 %copy.15 = f32[2,28,28,128]{3,0,2,1:T(2,128)} copy(f32[2,28,28,128]{3,2,1,0:T(8,128)} %shard_map.75) | data formatting | bytes 1605632 | tf_op jit(solution)/shard_map/pallas_call | solution.py:555
  (1 shorter events, 0.0 us)
Async XLA Ops:
  0.0 40.8 %slice-start = ((s8[5167104]{0:T(1024)(128)(4,1)}), s8[4194304]{0:T(1024)(128)(4,1)S(1)}, s32[]{:S(2)}) async-start(s8[5167104]{0:T(1024)(128)(4,1)} %bitcast.10), calls=%async_computation | async-start | bytes 8388608
  2.6 38.3 %slice-start.1 = ((s8[5167104]{0:T(1024)(128)(4,1)}), s8[972800]{0:T(1024)(128)(4,1)S(1)}, s32[]{:S(2)}) async-start(s8[5167104]{0:T(1024)(128)(4,1)} %bitcast.10), calls=%async_computation.1 | async-start | bytes 1945600
  40.9 4.0 %copy-start.1 = (f32[6,3,31]{2,1,0:T(4,128)S(1)}, f32[6,3,31]{2,1,0:T(4,128)}, u32[]{:S(2)}) copy-start(f32[6,3,31]{2,1,0:T(4,128)} %param.9) | copy-start | bytes 6700
  45.5 102.0 %copy-start = (f32[2,28,28,128]{3,0,2,1:T(2,128)S(1)}, f32[2,28,28,128]{3,0,2,1:T(2,128)}, u32[]{:S(2)}) copy-start(f32[2,28,28,128]{3,0,2,1:T(2,128)} %param.7) | copy-start | bytes 2408452
  45.5 103.1 %copy-start.2 = (s32[1,1,6]{2,1,0:T(1,128)S(1)}, s32[1,1,6]{2,1,0:T(1,128)}, u32[]{:S(2)}) copy-start(s32[1,1,6]{2,1,0:T(1,128)} %param.13) | copy-start | bytes 76

commit v2 on v1

--- a/solution.py
+++ b/solution.py
@@ -255,12 +255,12 @@
     p, r, low = p[:UP], r[:UP], low[:UP]
     cx[...] = pieces(band(lambda k: tap(0, k), taps, p - r + 2 * halo, (r < px) & (p < bx)), low)
     cy[...] = pieces(band(lambda k: tap(1, k), taps, p - r + 2 * halo, (r < py) & (p < by)), low)
-    row, w = iota((2 * nz, nz), 0), iota((2 * nz, nz), 1)
-    z = jnp.where(row >= nz, row - nz, row)
-    fz[...] = pieces(band(lambda k: tap(2, k), taps, z - w + halo, w < nz), row >= nz)
-    back = band(lambda k: tap(2, k), taps, w - z + halo, w < nz)
-    hi, lo = split(back)
-    cz[...] = jnp.concatenate([hi, lo], axis=1)
+    z, w = iota((nz, nz), 0), iota((nz, nz), 1)
+    hi, lo = split(band(lambda k: tap(2, k), taps, z - w + halo, w < nz))
+    fz[...] = jnp.concatenate([hi, lo], axis=0)
+    hi, lo = split(band(lambda k: tap(2, k), taps, w - z + halo, w < nz))
+    back = jnp.concatenate([hi, lo], axis=1)
+    cz[...] = jnp.concatenate([back, back], axis=0)
 
 
 def stack(a, b):
@@ -275,60 +275,68 @@
     return jnp.dot(a, b, preferred_element_type=F32)
 
 
-def job(block, view, backdrop, dims, mats, s1, s2, s3, emit):
+def in_groups(count, size, body):
+    full = count // size
+    if full:
+
+        def step(i, _):
+            body(i * size, size)
+            return 0
+
+        lax.fori_loop(0, full, step, 0)
+    if count % size:
+        body(full * size, count % size)
+
+
+def job(block, view, backdrop, dims, mats, s1, s2, emit):
     fx, fy, cx, cy, fz, cz = mats
     taps, halo, bx, by, nz = dims
     px, py = bx + 2 * halo, by + 2 * halo
-    chunk = 8
-
-    def first(i, _):
-        e = block(i * chunk, chunk).reshape(chunk * ROWS, nz)
+
+    def put(ref, line, pitch, size, value):
+        ref[pl.ds(pl.multiple_of(line * pitch, 8), size), :] = value[:, :nz]
+        ref[pl.ds(pl.multiple_of((line + 1) * pitch, 8), size), :] = value[:, nz:]
+
+    def first(y, count):
+        e = block(y, count).reshape(count * ROWS, nz)
         t = dot(jnp.concatenate([e, e], axis=1), fz[...])
-        for j in range(0, chunk, 2):
-            a, b = t[j * ROWS : (j + 1) * ROWS], t[(j + 1) * ROWS : (j + 2) * ROWS]
-            u = dot(fx[...], stack(a, b))
-            y = i * chunk + j
-            s1[pl.ds(pl.multiple_of(y * PITCH1, 8), ROWS), :] = u[:, :nz]
-            s1[pl.ds(pl.multiple_of((y + 1) * PITCH1, 8), ROWS), :] = u[:, nz:]
-        return 0
-
-    lax.fori_loop(0, ROWS // chunk, first, 0)
-
-    def second(i, _):
-        x = 2 * i
-        a = s1[pl.ds(x, ROWS, PITCH1), :]
-        b = s1[pl.ds(x + 1, ROWS, PITCH1), :]
-        predicted = dot(fy[...], stack(a, b)) + backdrop
+        lines = [t[j * ROWS : (j + 1) * ROWS] for j in range(count)]
+        done = [dot(fx[...], stack(lines[j], lines[j + 1])) for j in range(0, count, 2)]
+        for j, u in enumerate(done):
+            put(s1, y + 2 * j, PITCH1, ROWS, u)
+
+    in_groups(ROWS, 8, first)
+
+    def second(pair, count):
         pad = jnp.zeros((ROWS - py, nz), F32)
-        va = jnp.concatenate([view(x).astype(F32), pad], axis=0)
-        vb = jnp.concatenate([view(x + 1).astype(F32), pad], axis=0)
-        f = dot(cy[...], stack(va / predicted[:, :nz], vb / predicted[:, nz:]))
-        s2[pl.ds(pl.multiple_of(x * PITCH2, 8), UP), :] = f[:, :nz]
-        s2[pl.ds(pl.multiple_of((x + 1) * PITCH2, 8), UP), :] = f[:, nz:]
-        return 0
-
-    lax.fori_loop(0, px // 2, second, 0)
-
-    def third(i, _):
-        y = 2 * i
-        a = s2[pl.ds(y, ROWS, PITCH2), :]
-        b = s2[pl.ds(y + 1, ROWS, PITCH2), :]
-        f = dot(cx[...], stack(a, b))
-        s3[pl.ds(pl.multiple_of(y * UP, 8), UP), :] = f[:, :nz]
-        s3[pl.ds(pl.multiple_of((y + 1) * UP, 8), UP), :] = f[:, nz:]
-        return 0
-
-    lax.fori_loop(0, by // 2, third, 0)
-    piece = by * UP // 4
-
-    def fourth(i, _):
-        rows = pl.ds(pl.multiple_of(i * piece, 8), piece)
-        hi, lo = split(s3[rows, :])
+        done = []
+        for j in range(count):
+            x = 2 * (pair + j)
+            a = s1[pl.ds(x, ROWS, PITCH1), :]
+            b = s1[pl.ds(x + 1, ROWS, PITCH1), :]
+            predicted = dot(fy[...], stack(a, b)) + backdrop
+            va = jnp.concatenate([view(x).astype(F32), pad], axis=0)
+            vb = jnp.concatenate([view(x + 1).astype(F32), pad], axis=0)
+            done.append((va / predicted[:, :nz], vb / predicted[:, nz:]))
+        done = [dot(cy[...], stack(a, b)) for a, b in done]
+        for j, f in enumerate(done):
+            put(s2, 2 * (pair + j), PITCH2, UP, f)
+
+    in_groups(px // 2, 4, second)
+
+    def third(pair, count):
+        done = []
+        for j in range(count):
+            y = 2 * (pair + j)
+            a = s2[pl.ds(y, ROWS, PITCH2), :]
+            b = s2[pl.ds(y + 1, ROWS, PITCH2), :]
+            done.append(dot(cx[...], stack(a, b)))
+        f = jnp.concatenate([v for f in done for v in (f[:, :nz], f[:, nz:])], axis=0)
+        hi, lo = split(f)
         out = dot(jnp.concatenate([hi, lo], axis=1), cz[...])
-        emit(rows, out[:, :nz] + out[:, nz:])
-        return 0
-
-    lax.fori_loop(0, 4, fourth, 0)
+        emit(pl.ds(pl.multiple_of(pair * 2 * UP, 8), count * 2 * UP), out[:, :nz] + out[:, nz:])
+
+    in_groups(by // 2, 7, third)
 
 
 def job_scratch(by, nz):
@@ -341,12 +349,11 @@
         pltpu.VMEM((2 * nz, 2 * nz), BF16),
         pltpu.VMEM((ROWS * PITCH1, nz), F32),
         pltpu.VMEM((ROWS * PITCH2, nz), F32),
-        pltpu.VMEM((by * UP, nz), F32),
     ]
 
 
 def jobs_kernel(n, dims, gathered, views, psf, background, bricks, slot_views, contrib, *scratch):
-    mats, (s1, s2, s3) = scratch[:6], scratch[6:]
+    mats, (s1, s2) = scratch[:6], scratch[6:]
     taps, halo, bx, by, nz = dims
     s, c = pl.program_id(0), pl.program_id(1)
     brick, view = bricks[s], slot_views[s]
@@ -372,7 +379,7 @@
         def _():
             contrib[brick, c, rows, :] += value
 
-    job(block, lambda x: views[0, 0, x], background[view], dims, mats, s1, s2, s3, emit)
+    job(block, lambda x: views[0, 0, x], background[view], dims, mats, s1, s2, emit)
 
 
 class Scatter:

time: 184 us -> 136 us (0.74)
  Pallas kernels: 172 us -> 123 us
    pallas_call x1, Pallas kernels: 102 us -> 53.3 us  [on_device(): pl.pallas_call(functools.partial(jobs_kernel, n, dims), grid=(slots, chan...]
where the time goes in v2:
time: 136 us; the launch traced here: 135 us
  Pallas kernels  123 us (90%)
  local copies, waits for them, and re-layouts  8.58 us (6%)
  other arithmetic  3 us (2%)
    pallas_call x1, Pallas kernels, on_device(): pl.pallas_call(functools.partial(jobs_kernel, n, dims), grid=(slots, chan...  53.3 us
    pallas_call x1, Pallas kernels, on_device(): pl.pallas_call(functools.partial(gather_kernel, n, nv, by, halo), out_sha...  38.3 us
    pallas_call x1, Pallas kernels, on_device(): pl.pallas_call(functools.partial(scatter_kernel, n, nv), out_shape=jax.Sh...  31.6 us
    unnamed x12, local copies, waits for them, and re-layouts  5.03 us

profile of v2, /device:TPU:0, one launch (start us, length us, event | category | flops | bytes accessed | tf_op | source)
XLA Modules:
  0.0 135.4 jit_solution(17193888181557910482)
XLA Ops:
  0.0 0.0 slice-start
  0.0 1.6 %convert_element_type.6 = bf16[2,28,28,128]{3,0,2,1:T(2,128)(2,1)S(1)} convert(f32[2,28,28,128]{3,0,2,1:T(2,128)} %param.7) | non-fusion elementwise | flops 200704 | bytes 1204224 | tf_op jit(solution)/shard_map/convert_element_type | solution.py:532
  1.6 0.1 copy.19
  1.7 0.1 fusion
  1.8 0.8 pad_maximum_fusion.wire
  2.6 0.0 slice-start.1
  2.6 38.3 %shard_map.73.gathered = bf16[2,260,64,128]{3,2,1,0:T(8,128)(2,1)} custom-call(bf16[2,28,32,128]{3,2,1,0:T(8,128)(2,1)} %pad_maximum_fusion.wire), custom_call_target="tpu_custom_call" | custom-call | tf_op jit(solution)/shard_map/pallas_call | solution.py:536
  40.8 0.0 slice-done
  40.9 0.0 slice-done.1
  40.9 0.0 copy-start.1
  40.9 3.9 %copy.18 = bf16[1,1,3,2,58,58,128]{6,5,4,3,2,1,0:T(8,128)(2,1)} copy(bf16[1,1,3,2,58,58,128]{6,3,5,4,2,1,0:T(2,128)(2,1)S(1)} %bitcast.11) | data formatting | bytes 10334208 | tf_op args[1]
  44.8 0.0 copy-done.1
  44.8 0.7 reshape.6.psf
  45.5 0.0 copy-start
  45.5 0.0 copy-start.2
  45.5 53.3 %shard_map.74.contrib = f32[8,2,896,128]{3,2,1,0:T(8,128)} custom-call(bf16[2,260,64,128]{3,2,1,0:T(8,128)(2,1)} %shard_map.73.gathered, bf16[3,2,58,58,128]{4,3,2,1,0:T(8,128)(2,1)} %bitcast.9, f32[558]{0:T(1024)} %reshape.6.psf, f32[6]{0:T(128)} %background.1, s32[3]{0:T(128)} %bitcast.13, s32[3]{0:T(128)} %bitcast.14), custom_call_target="tpu_custom_call" | custom-call | tf_op jit(solution)/shard_map/pallas_call | solution.py:545
  98.8 0.0 copy-done
  98.8 1.1 copy.14.estimate
  99.9 0.0 copy-done.2
  99.9 0.6 reduce_sum.9
  101.2 31.6 %shard_map.75 = f32[2,28,28,128]{3,2,1,0:T(8,128)} custom-call(f32[8,2,896,128]{3,2,1,0:T(8,128)} %shard_map.74.contrib, f32[2,28,28,128]{3,2,1,0:T(8,128)} %copy.14.estimate, f32[1]{0:T(128)} %bitcast.4.seen_ref), custom_call_target="tpu_custom_call" | custom-call | tf_op jit(solution)/shard_map/pallas_call | solution.py:562
  132.8 2.7 %copy.15 = f32[2,28,28,128]{3,0,2,1:T(2,128)} copy(f32[2,28,28,128]{3,2,1,0:T(8,128)} %shard_map.75) | data formatting | bytes 1605632 | tf_op jit(solution)/shard_map/pallas_call | solution.py:562
  (1 shorter events, 0.0 us)
Async XLA Ops:
  0.0 40.8 %slice-start = ((s8[5167104]{0:T(1024)(128)(4,1)}), s8[4194304]{0:T(1024)(128)(4,1)S(1)}, s32[]{:S(2)}) async-start(s8[5167104]{0:T(1024)(128)(4,1)} %bitcast.10), calls=%async_computation | async-start | bytes 8388608
  2.6 38.3 %slice-start.1 = ((s8[5167104]{0:T(1024)(128)(4,1)}), s8[972800]{0:T(1024)(128)(4,1)S(1)}, s32[]{:S(2)}) async-start(s8[5167104]{0:T(1024)(128)(4,1)} %bitcast.10), calls=%async_computation.1 | async-start | bytes 1945600
  40.9 4.0 %copy-start.1 = (f32[6,3,31]{2,1,0:T(4,128)S(1)}, f32[6,3,31]{2,1,0:T(4,128)}, u32[]{:S(2)}) copy-start(f32[6,3,31]{2,1,0:T(4,128)} %param.9) | copy-start | bytes 6700
  45.5 53.3 %copy-start = (f32[2,28,28,128]{3,0,2,1:T(2,128)S(1)}, f32[2,28,28,128]{3,0,2,1:T(2,128)}, u32[]{:S(2)}) copy-start(f32[2,28,28,128]{3,0,2,1:T(2,128)} %param.7) | copy-start | bytes 2408452
  45.5 54.4 %copy-start.2 = (s32[1,1,6]{2,1,0:T(1,128)S(1)}, s32[1,1,6]{2,1,0:T(1,128)}, u32[]{:S(2)}) copy-start(s32[1,1,6]{2,1,0:T(1,128)} %param.13) | copy-start | bytes 76

commit v3 on v2

--- a/solution.py
+++ b/solution.py
@@ -63,7 +63,7 @@
 
     def slab(self, c, b, part):
         start, size = ((HB, 2 * HB), (0, HB), (3 * HB, HB))[part]
-        return self.out.at[c, pl.ds(self.halo + self.by * b, self.by), pl.ds(start, size), :]
+        return self.out[c].at[pl.ds(self.halo + self.by * b, self.by), pl.ds(start, size), :]
 
     def copy(self, src, dst, s, r, dev):
         return pltpu.make_async_remote_copy(
@@ -92,7 +92,7 @@
         if k == 0:
             src = self.wire.at[c, :, pl.ds(first, HB), :]
         else:
-            src = self.out.at[c, pl.ds(self.halo + self.by * b, self.by), pl.ds(HB + first, HB), :]
+            src = self.out[c].at[pl.ds(self.halo + self.by * b, self.by), pl.ds(HB + first, HB), :]
         side = 0 if up else 1
         return self.copy(
             src,
@@ -115,35 +115,27 @@
             act(self.to_view(c, k, False))
 
     def zeros(self):
-        count = self.out.shape[1]
+        count = self.out[0].shape[0]
         last = self.halo + self.by * self.n
 
-        def clear(where):
-            self.out[where] = jnp.zeros(self.out.at[where].shape, BF16)
-
-        def edge(i, _):
-            for c in range(2):
-                self.out[c, pl.ds(i, 1)] = jnp.zeros((1,) + self.out.shape[2:], BF16)
-            return 0
-
-        lax.fori_loop(0, self.halo, edge, 0)
-        lax.fori_loop(last, count, edge, 0)
-
-        def rows(start):
+        def fill(low, high, start, size):
             def body(i, _):
-                for c in range(2):
-                    self.out[c, pl.ds(i, 1), pl.ds(start, HB), :] = jnp.zeros((1, HB, 128), BF16)
+                for ref in self.out:
+                    ref[pl.ds(i, 1), pl.ds(start, size), :] = jnp.zeros((1, size, ref.shape[2]), BF16)
                 return 0
 
-            lax.fori_loop(self.halo, last, body, 0)
+            lax.fori_loop(low, high, body, 0)
+
+        fill(0, self.halo, 0, ROWS)
+        fill(last, count, 0, ROWS)
 
         @pl.when(self.v == 0)
         def _():
-            rows(0)
+            fill(self.halo, last, 0, HB)
 
         @pl.when(self.v == self.nv - 1)
         def _():
-            rows(3 * HB)
+            fill(self.halo, last, 3 * HB, HB)
 
     def begin(self, c):
         for k in range(1, self.n // 2):
@@ -158,6 +150,7 @@
             self.views(c, k, lambda d: d.start())
             self.to_sib(c, k, 0).start()
 
+    def forward_sides(self, c):
         def side(k, part, when):
             @pl.when(when)
             def _():
@@ -201,19 +194,6 @@
     q = n // 2
     dma = pltpu.SemaphoreType.DMA
     return [dma((2, q)), dma((2, q)), dma((2, q, 2)), dma((2, q, 2)), dma((2, q, 3)), dma((2, q, 3)), dma((2,))]
-
-
-def gather_kernel(n, nv, by, halo, wire, out, *sems):
-    g = Gather(n, nv, by, halo, wire, out, sems)
-    greet(n, nv, True)
-    g.begin(0)
-    g.begin(1)
-    g.zeros()
-    for c in range(2):
-        g.forward(c)
-    for c in range(2):
-        g.arrive(c)
-        g.finish(c)
 
 
 def iota(shape, dim):
@@ -339,60 +319,45 @@
     in_groups(by // 2, 7, third)
 
 
-def job_scratch(by, nz):
+def job_scratch(slots, nz):
     return [
-        pltpu.VMEM((ROWS, 3 * ROWS), BF16),
-        pltpu.VMEM((ROWS, 3 * ROWS), BF16),
-        pltpu.VMEM((UP, 3 * ROWS), BF16),
-        pltpu.VMEM((UP, 3 * ROWS), BF16),
-        pltpu.VMEM((2 * nz, nz), BF16),
-        pltpu.VMEM((2 * nz, 2 * nz), BF16),
+        pltpu.VMEM((slots, ROWS, 3 * ROWS), BF16),
+        pltpu.VMEM((slots, ROWS, 3 * ROWS), BF16),
+        pltpu.VMEM((slots, UP, 3 * ROWS), BF16),
+        pltpu.VMEM((slots, UP, 3 * ROWS), BF16),
+        pltpu.VMEM((slots, 2 * nz, nz), BF16),
+        pltpu.VMEM((slots, 2 * nz, 2 * nz), BF16),
         pltpu.VMEM((ROWS * PITCH1, nz), F32),
         pltpu.VMEM((ROWS * PITCH2, nz), F32),
     ]
 
 
-def jobs_kernel(n, dims, gathered, views, psf, background, bricks, slot_views, contrib, *scratch):
-    mats, (s1, s2) = scratch[:6], scratch[6:]
-    taps, halo, bx, by, nz = dims
-    s, c = pl.program_id(0), pl.program_id(1)
-    brick, view = bricks[s], slot_views[s]
-
-    @pl.when((s == 0) & (c == 0))
-    def _():
-        s2[...] = jnp.zeros_like(s2)
-
-    @pl.when(c == 0)
-    def _():
-        build_bands(lambda a, k: psf[(view * 3 + a) * taps + k], dims, mats)
-
-    def block(y, count):
-        return gathered[c, pl.ds(brick * by + y, count)]
-
-    def emit(rows, value):
-        @pl.when(s == 0)
-        def _():
-            for o in range(n):
-                contrib[o, c, rows, :] = jnp.where(brick == o, value, 0.0)
-
-        @pl.when(s > 0)
-        def _():
-            contrib[brick, c, rows, :] += value
-
-    job(block, lambda x: views[0, 0, x], background[view], dims, mats, s1, s2, emit)
-
-
 class Scatter:
-    def __init__(self, n, by, nz, contrib, rx1, code, scale, code_in, scale_in, sems):
+    def __init__(self, n, by, nz, bricks, factors, tx1, rx1, code, scale, code_in, scale_in, final, sems):
         self.n, self.nz, self.rows = n, nz, by * UP
-        self.contrib, self.rx1 = contrib, rx1
+        self.bricks, self.factors, self.tx1, self.rx1, self.final = bricks, factors, tx1, rx1, final
         self.code, self.scale, self.code_in, self.scale_in = code, scale, code_in, scale_in
         self.s1, self.r1, self.s2, self.r2 = sems
         self.t, self.v, self.sib = place(n)
 
+    def own(self, c, o, rows):
+        parts = [
+            jnp.where(self.bricks[s] == o, self.factors[s, c, rows, :], 0.0)
+            for s in range(self.factors.shape[0])
+        ]
+        return sum(parts[1:], parts[0])
+
+    def loop(self, body, init=0):
+        piece = 128
+
+        def step(i, carry):
+            return body(pl.ds(pl.multiple_of(i * piece, 16), piece), carry)
+
+        return lax.fori_loop(0, self.rows // piece, step, init)
+
     def pair(self, c, j):
         return pltpu.make_async_remote_copy(
-            src_ref=self.contrib.at[same(self.sib, j, self.n), c],
+            src_ref=self.tx1.at[j, c],
             dst_ref=self.rx1.at[j, c],
             send_sem=self.s1.at[j, c],
             recv_sem=self.r1.at[j, c],
@@ -411,60 +376,59 @@
             device_id_type=MESH,
         )
 
-    def order(self):
-        return list(range(1, self.n // 2)) + [0]
-
     def begin(self, c):
-        for j in self.order():
+        for j in list(range(1, self.n // 2)) + [0]:
+            o = same(self.sib, j, self.n)
+
+            def fill(rows, _):
+                self.tx1[j, c, rows, :] = self.own(c, o, rows)
+                return 0
+
+            self.loop(fill)
             self.pair(c, j).start()
 
     def send(self, c):
-        piece = 128
         for j in range(1, self.n // 2):
             self.pair(c, j).wait_recv()
             o = same(self.t, j, self.n)
 
-            def add(i, top):
-                rows = pl.ds(pl.multiple_of(i * piece, 8), piece)
-                value = self.contrib[o, c, rows, :] + self.rx1[j, c, rows, :]
+            def add(rows, top):
+                value = self.own(c, o, rows) + self.rx1[j, c, rows, :]
                 self.rx1[j, c, rows, :] = value
-                return jnp.maximum(top, jnp.max(value.reshape(piece // 8, 8, self.nz), axis=0))
-
-            top = lax.fori_loop(0, self.rows // piece, add, jnp.zeros((8, self.nz), F32))
+                return jnp.maximum(top, jnp.max(value.reshape(-1, 8, self.nz), axis=0))
+
+            top = self.loop(add, jnp.zeros((8, self.nz), F32))
             top = jnp.max(top, axis=0, keepdims=True)
             top = jnp.where(top > 0.0, top, 1.0)
             self.scale[j, c] = jnp.broadcast_to(top, (8, self.nz))
             gain = 1.0 / top
 
-            def pack(i, _):
-                rows = pl.ds(pl.multiple_of(i * piece, 16), piece)
+            def pack(rows, _):
                 level = jnp.minimum(self.rx1[j, c, rows, :] * gain * 65535.0, 65535.0)
                 whole = jnp.round(level).astype(jnp.int32) - 32768
                 self.code[j, c, rows, :] = whole.astype(jnp.int16)
                 return 0
 
-            lax.fori_loop(0, self.rows // piece, pack, 0)
+            self.loop(pack)
             self.chip(c, j, 0).start()
             self.chip(c, j, 1).start()
 
     def total(self, c):
-        piece = 128
         q = self.n // 2
         self.pair(c, 0).wait_recv()
         for j in range(1, q):
             self.chip(c, j, 0).wait_recv()
             self.chip(c, j, 1).wait_recv()
 
-        def add(i, _):
-            rows = pl.ds(pl.multiple_of(i * piece, 16), piece)
-            value = self.contrib[self.t, c, rows, :] + self.rx1[0, c, rows, :]
+        def add(rows, _):
+            value = self.own(c, self.t, rows) + self.rx1[0, c, rows, :]
             for j in range(1, q):
                 level = self.code_in[j, c, rows, :].astype(jnp.int32).astype(F32) + 32768.0
                 value = value + level * (self.scale_in[j, c, 0:1, :] * (1.0 / 65535.0))
-            self.rx1[0, c, rows, :] = value
+            self.final[rows, :] = value
             return 0
 
-        lax.fori_loop(0, self.rows // piece, add, 0)
+        self.loop(add)
 
     def finish(self, c):
         for j in range(self.n // 2):
@@ -474,20 +438,24 @@
                 self.chip(c, j, 1).wait_send()
 
 
-def scatter_scratch(n, by, nz):
+def scatter_scratch(n, slots, by, nz):
     q, rows = n // 2, by * UP
-    dma = pltpu.SemaphoreType.DMA
     return [
+        pltpu.VMEM((slots, 2, rows, nz), F32),
+        pltpu.VMEM((q, 2, rows, nz), F32),
         pltpu.VMEM((q, 2, rows, nz), F32),
         pltpu.VMEM((q, 2, rows, nz), jnp.int16),
         pltpu.VMEM((q, 2, 8, nz), F32),
         pltpu.VMEM((q, 2, rows, nz), jnp.int16),
         pltpu.VMEM((q, 2, 8, nz), F32),
-        dma((q, 2)),
-        dma((q, 2)),
-        dma((q, 2, 2)),
-        dma((q, 2, 2)),
+        pltpu.VMEM((rows, nz), F32),
     ]
+
+
+def scatter_sems(n):
+    q = n // 2
+    dma = pltpu.SemaphoreType.DMA
+    return [dma((q, 2)), dma((q, 2)), dma((q, 2, 2)), dma((q, 2, 2))]
 
 
 def update(c, estimate, out, total, seen):
@@ -500,27 +468,98 @@
     lax.fori_loop(0, bx, body, 0)
 
 
-def scatter_kernel(n, nv, contrib, estimate, seen_ref, out, rx1, code, scale, code_in, scale_in, *rest):
-    by, nz = estimate.shape[2:]
-    sems, final = rest[:4], rest[4]
-    s = Scatter(n, by, nz, contrib, rx1, code, scale, code_in, scale_in, sems)
-    greet(n, nv, False)
-    s.begin(0)
-    s.begin(1)
-    seen = seen_ref[0]
+def kernel(n, nv, dims, wire, estimate, views, psf, background, bricks, slot_views, crossing, out, *scratch):
+    taps, halo, bx, by, nz = dims
+    slots = views.shape[0]
+    take = lambda count: [scratch.pop(0) for _ in range(count)]
+    scratch = list(scratch)
+    blocks, (seen_views, views_sem), mats, (s1, s2), parts = take(2), take(2), take(6), take(2), take(8)
+    gather_all, scatter_all = take(7), take(4)
+    g = Gather(n, nv, by, halo, wire, blocks, gather_all)
+    f = Scatter(n, by, nz, bricks, *parts, scatter_all)
+    factors = parts[0]
+
+    def fetch(s, c):
+        return pltpu.make_async_copy(views.at[s, c], seen_views.at[s, c], views_sem.at[s, c])
+
     for c in range(2):
-        s.send(c)
+        for s in range(slots):
+            fetch(s, c).start()
+    greet(n, nv, True)
+    g.begin(0)
+    g.zeros()
+    s2[...] = jnp.zeros_like(s2)
+
+    def bands(s, _):
+        view = slot_views[s]
+        build_bands(lambda a, k: psf[(view * 3 + a) * taps + k], dims, [m.at[s] for m in mats])
+        return 0
+
+    lax.fori_loop(0, slots, bands, 0)
+    g.forward(0)
+    g.begin(1)
+    g.forward_sides(0)
+    g.arrive(0)
+
+    def run(c, s):
+        brick = bricks[s]
+        fetch(s, c).wait()
+
+        def emit(rows, value):
+            factors[s, c, rows, :] = value
+
+        job(
+            lambda y, count: blocks[c][pl.ds(brick * by + y, count)],
+            lambda x: seen_views[s, c, x],
+            background[slot_views[s]],
+            dims,
+            [m.at[s] for m in mats],
+            s1,
+            s2,
+            emit,
+        )
+
+    def beside(c, s):
+        if c == 0:
+
+            @pl.when(s == 0)
+            def _():
+                g.forward(1)
+
+            @pl.when(s == 1)
+            def _():
+                g.forward_sides(1)
+
+        else:
+
+            @pl.when(s == 0)
+            def _():
+                f.send(0)
+
     for c in range(2):
-        s.total(c)
-
-        def move(i, _):
-            rows = pl.ds(pl.multiple_of(i * 128, 8), 128)
-            final[rows, :] = rx1[0, c, rows, :]
+
+        def step(s, _):
+            run(c, s)
+            beside(c, s)
             return 0
 
-        lax.fori_loop(0, by * UP // 128, move, 0)
-        update(c, estimate, out, final, seen)
-        s.finish(c)
+        lax.fori_loop(0, slots, step, 0)
+        if c == 0:
+            g.arrive(1)
+        f.begin(c)
+    seen = crossing[0]
+    for k in range(1, crossing.shape[0]):
+        seen = seen + crossing[k]
+    seen = seen.astype(F32)
+    f.total(0)
+    update(0, estimate, out, f.final, seen)
+    f.send(1)
+    for c in range(2):
+        g.finish(c)
+    f.total(1)
+    update(1, estimate, out, f.final, seen)
+    for c in range(2):
+        f.finish(c)
 
 
 def on_device(n, nv, estimate, view_data, psf, background, slot_brick, slot_view, intersection):
@@ -532,41 +571,30 @@
     est_wire = jnp.swapaxes(estimate.astype(BF16), 1, 2)
     wire = jnp.concatenate([est_wire[:, :, :HB], est_wire[:, :, bx - HB :]], axis=2)
     count = 2 * halo + by * n + ROWS - py
-    limit = 56 * 1024 * 1024
-    gathered = pl.pallas_call(
-        functools.partial(gather_kernel, n, nv, by, halo),
-        out_shape=jax.ShapeDtypeStruct((channels, count, ROWS, nz), BF16),
-        in_specs=[VMEM],
+    return pl.pallas_call(
+        functools.partial(kernel, n, nv, dims),
+        out_shape=jax.ShapeDtypeStruct(estimate.shape, F32),
+        in_specs=[VMEM, VMEM, pl.BlockSpec(memory_space=pl.ANY)] + [SMEM] * 5,
         out_specs=VMEM,
-        scratch_shapes=gather_sems(n),
-        compiler_params=pltpu.CompilerParams(collective_id=0, has_side_effects=True, vmem_limit_bytes=limit),
-    )(wire)
-    whole = lambda *shape: pl.BlockSpec(shape, lambda s, c: (0,) * len(shape))
-    contrib = pl.pallas_call(
-        functools.partial(jobs_kernel, n, dims),
-        grid=(slots, channels),
-        out_shape=jax.ShapeDtypeStruct((n, channels, by * UP, nz), F32),
-        in_specs=[
-            whole(channels, count, ROWS, nz),
-            pl.BlockSpec((1, 1, px, py, nz), lambda s, c: (s, c, 0, 0, 0)),
-            SMEM,
-            SMEM,
-            SMEM,
-            SMEM,
-        ],
-        out_specs=whole(n, channels, by * UP, nz),
-        scratch_shapes=job_scratch(by, nz),
-        compiler_params=pltpu.CompilerParams(vmem_limit_bytes=limit),
-    )(gathered, view_data[0, 0], psf.reshape(-1), background, slot_brick[0, 0], slot_view[0, 0])
-    seen = jnp.sum(intersection[0, 0]).astype(F32).reshape(1)
-    return pl.pallas_call(
-        functools.partial(scatter_kernel, n, nv),
-        out_shape=jax.ShapeDtypeStruct(estimate.shape, F32),
-        in_specs=[VMEM, VMEM, SMEM],
-        out_specs=VMEM,
-        scratch_shapes=scatter_scratch(n, by, nz) + [pltpu.VMEM((by * UP, nz), F32)],
-        compiler_params=pltpu.CompilerParams(collective_id=1, has_side_effects=True, vmem_limit_bytes=limit),
-    )(contrib, estimate, seen)
+        scratch_shapes=[pltpu.VMEM((count, ROWS, nz), BF16)] * 2
+        + [pltpu.VMEM((slots, channels, px, py, nz), BF16), pltpu.SemaphoreType.DMA((slots, channels))]
+        + job_scratch(slots, nz)
+        + scatter_scratch(n, slots, by, nz)
+        + gather_sems(n)
+        + scatter_sems(n),
+        compiler_params=pltpu.CompilerParams(
+            collective_id=0, has_side_effects=True, vmem_limit_bytes=60 * 1024 * 1024
+        ),
+    )(
+        wire,
+        estimate,
+        view_data[0, 0],
+        psf.reshape(-1),
+        background,
+        slot_brick[0, 0],
+        slot_view[0, 0],
+        intersection[0, 0],
+    )
 
 
 def solution(mesh):

time: 136 us -> 101 us (0.74)
  Pallas kernels: 123 us -> 87.2 us
  local copies, waits for them, and re-layouts: 8.58 us -> 10.4 us
    pallas_call x3 -> x1, Pallas kernels: 123 us -> 87.2 us  [on_device(): pl.pallas_call(functools.partial(kernel, n, nv, dims), out_shape=jax.Shap...]
    unnamed x12 -> x4, local copies, waits for them, and re-layouts: 5.03 us -> 6.19 us
where the time goes in v3:
time: 101 us; the launch traced here: 100 us
  Pallas kernels  87.2 us (86%)
  local copies, waits for them, and re-layouts  10.4 us (10%)
  other arithmetic  2.36 us (2%)
    pallas_call x1, Pallas kernels, on_device(): pl.pallas_call(functools.partial(kernel, n, nv, dims), out_shape=jax.Shap...  87.2 us
    unnamed x4, local copies, waits for them, and re-layouts  6.19 us
    pallas_call x1, local copies, waits for them, and re-layouts, on_device(): pl.pallas_call(functools.partial(kernel, n, nv, dims), out_shape=jax.Shap...  2.69 us

profile of v3, /device:TPU:0, one launch (start us, length us, event | category | flops | bytes accessed | tf_op | source)
XLA Modules:
  0.0 100.1 jit_solution(17254539708812679681)
XLA Ops:
  0.0 1.4 %reshape.3.psf = f32[558]{0:T(1024)} reshape(f32[6,3,31]{2,1,0:T(4,128)} %param.9) | data formatting | bytes 4464 | tf_op jit(solution)/shard_map/reshape | solution.py:592
  1.4 0.0 copy-start
  1.4 1.6 %convert_element_type.3 = bf16[2,28,28,128]{3,0,2,1:T(2,128)(2,1)S(1)} convert(f32[2,28,28,128]{3,0,2,1:T(2,128)} %param.7) | non-fusion elementwise | flops 200704 | bytes 1204224 | tf_op jit(solution)/shard_map/convert_element_type | solution.py:571
  3.0 0.1 copy.19
  3.0 0.1 fusion
  3.1 0.8 pad_maximum_fusion.wire
  3.9 2.2 %copy.14.estimate = f32[2,28,28,128]{3,2,1,0:T(8,128)} copy(f32[2,28,28,128]{3,0,2,1:T(2,128)} %param.7) | data formatting | bytes 1605632 | tf_op args[0]
  6.1 0.0 copy-done
  6.1 4.0 %copy.18 = bf16[1,1,3,2,58,58,128]{6,5,4,3,2,1,0:T(8,128)(2,1)} copy(bf16[1,1,3,2,58,58,128]{6,3,5,4,2,1,0:T(2,128)(2,1)S(1)} %copy-done) | data formatting | bytes 10334208 | tf_op args[1]
  10.1 87.2 %shard_map.73 = f32[2,28,28,128]{3,2,1,0:T(8,128)} custom-call(bf16[2,28,32,128]{3,2,1,0:T(8,128)(2,1)} %pad_maximum_fusion.wire, f32[2,28,28,128]{3,2,1,0:T(8,128)} %copy.14.estimate, bf16[3,2,58,58,128]{4,3,2,1,0:T(8,128)(2,1)} %bitcast.9, f32[558]{0:T(1024)} %reshape.3.psf, f32[6]{0:T(128)} %background.1, s32[3]{0:T(128)} %bitcast.11, s32[3]{0:T(128)} %bitcast.12, ...), custom_call_target="tpu_custom_call" | custom-call | tf_op jit(solution)/shard_map/pallas_call | solution.py:574
  97.4 2.7 %copy.15 = f32[2,28,28,128]{3,0,2,1:T(2,128)} copy(f32[2,28,28,128]{3,2,1,0:T(8,128)} %shard_map.73) | data formatting | bytes 1605632 | tf_op jit(solution)/shard_map/pallas_call | solution.py:574
Async XLA Ops:
  1.4 4.8 %copy-start = (bf16[1,1,3,2,58,58,128]{6,3,5,4,2,1,0:T(2,128)(2,1)S(1)}, bf16[1,1,3,2,58,58,128]{6,3,5,4,2,1,0:T(2,128)(2,1)}, u32[]{:S(2)}) copy-start(bf16[1,1,3,2,58,58,128]{6,3,5,4,2,1,0:T(2,128)(2,1)} %param.8) | copy-start | bytes 15501316

commit v4 on v3

--- a/solution.py
+++ b/solution.py
@@ -15,6 +15,7 @@
 UP = 32
 PITCH1 = 72
 PITCH2 = 40
+GROUP = 8
 VMEM = pl.BlockSpec(memory_space=pltpu.VMEM)
 SMEM = pl.BlockSpec(memory_space=pltpu.SMEM)
 
@@ -268,7 +269,7 @@
         body(full * size, count % size)
 
 
-def job(block, view, backdrop, dims, mats, s1, s2, emit):
+def job(c, block, view, backdrop, dims, mats, s1, s2, vf, emit):
     fx, fy, cx, cy, fz, cz = mats
     taps, halo, bx, by, nz = dims
     px, py = bx + 2 * halo, by + 2 * halo
@@ -285,24 +286,25 @@
         for j, u in enumerate(done):
             put(s1, y + 2 * j, PITCH1, ROWS, u)
 
-    in_groups(ROWS, 8, first)
+    in_groups(ROWS, 16, first)
 
     def second(pair, count):
-        pad = jnp.zeros((ROWS - py, nz), F32)
         done = []
+        line = 2 * py
+        vf[: count * 2 * line, :] = view(2 * pair, 2 * count).astype(F32)
         for j in range(count):
             x = 2 * (pair + j)
             a = s1[pl.ds(x, ROWS, PITCH1), :]
             b = s1[pl.ds(x + 1, ROWS, PITCH1), :]
             predicted = dot(fy[...], stack(a, b)) + backdrop
-            va = jnp.concatenate([view(x).astype(F32), pad], axis=0)
-            vb = jnp.concatenate([view(x + 1).astype(F32), pad], axis=0)
+            va = vf[pl.ds(2 * j * line + c, ROWS, 2), :]
+            vb = vf[pl.ds((2 * j + 1) * line + c, ROWS, 2), :]
             done.append((va / predicted[:, :nz], vb / predicted[:, nz:]))
         done = [dot(cy[...], stack(a, b)) for a, b in done]
         for j, f in enumerate(done):
             put(s2, 2 * (pair + j), PITCH2, UP, f)
 
-    in_groups(px // 2, 4, second)
+    in_groups(px // 2, GROUP, second)
 
     def third(pair, count):
         done = []
@@ -316,10 +318,10 @@
         out = dot(jnp.concatenate([hi, lo], axis=1), cz[...])
         emit(pl.ds(pl.multiple_of(pair * 2 * UP, 8), count * 2 * UP), out[:, :nz] + out[:, nz:])
 
-    in_groups(by // 2, 7, third)
-
-
-def job_scratch(slots, nz):
+    in_groups(by // 2, 14, third)
+
+
+def job_scratch(slots, py, nz):
     return [
         pltpu.VMEM((slots, ROWS, 3 * ROWS), BF16),
         pltpu.VMEM((slots, ROWS, 3 * ROWS), BF16),
@@ -329,6 +331,7 @@
         pltpu.VMEM((slots, 2 * nz, 2 * nz), BF16),
         pltpu.VMEM((ROWS * PITCH1, nz), F32),
         pltpu.VMEM((ROWS * PITCH2, nz), F32),
+        pltpu.VMEM((GROUP * 4 * py + 16, nz), F32),
     ]
 
 
@@ -458,41 +461,53 @@
     return [dma((q, 2)), dma((q, 2)), dma((q, 2, 2)), dma((q, 2, 2))]
 
 
-def update(c, estimate, out, total, seen):
-    bx, by = estimate.shape[1:3]
-
+def update(c, bx, by, estimate, out, total, seen):
     def body(u, _):
-        out[c, u] = estimate[c, u] * total[pl.ds(u, by, UP), :] / seen
+        where = pl.ds(u * 2 * by + c, by, 2)
+        out[where, :] = estimate[where, :] * total[pl.ds(u, by, UP), :] / seen
         return 0
 
     lax.fori_loop(0, bx, body, 0)
 
 
-def kernel(n, nv, dims, wire, estimate, views, psf, background, bricks, slot_views, crossing, out, *scratch):
+def round_wire(c, bx, by, estimate, wire):
+    def body(y, _):
+        for start, first in ((0, 0), (HB, bx - HB)):
+            rows = estimate[pl.ds(first * 2 * by + 2 * y + c, HB, 2 * by), :]
+            wire[c, y, start : start + HB, :] = rows.astype(BF16)
+        return 0
+
+    lax.fori_loop(0, by, body, 0)
+
+
+def kernel(n, nv, dims, estimate, views, psf, background, bricks, slot_views, crossing, out, *scratch):
     taps, halo, bx, by, nz = dims
     slots = views.shape[0]
     take = lambda count: [scratch.pop(0) for _ in range(count)]
     scratch = list(scratch)
-    blocks, (seen_views, views_sem), mats, (s1, s2), parts = take(2), take(2), take(6), take(2), take(8)
+    (wire,), blocks, (seen_views, views_sem) = take(1), take(2), take(2)
+    mats, (s1, s2, vf), parts = take(6), take(3), take(8)
     gather_all, scatter_all = take(7), take(4)
     g = Gather(n, nv, by, halo, wire, blocks, gather_all)
     f = Scatter(n, by, nz, bricks, *parts, scatter_all)
     factors = parts[0]
 
-    def fetch(s, c):
-        return pltpu.make_async_copy(views.at[s, c], seen_views.at[s, c], views_sem.at[s, c])
-
-    for c in range(2):
-        for s in range(slots):
-            fetch(s, c).start()
+    def fetch(s):
+        return pltpu.make_async_copy(views.at[s], seen_views.at[s], views_sem.at[s])
+
+    round_wire(0, bx, by, estimate, wire)
     greet(n, nv, True)
     g.begin(0)
+    for s in range(slots):
+        fetch(s).start()
+    round_wire(1, bx, by, estimate, wire)
     g.zeros()
     s2[...] = jnp.zeros_like(s2)
+    vf[...] = jnp.zeros_like(vf)
 
     def bands(s, _):
         view = slot_views[s]
-        build_bands(lambda a, k: psf[(view * 3 + a) * taps + k], dims, [m.at[s] for m in mats])
+        build_bands(lambda a, k: psf[view, a, k], dims, [m.at[s] for m in mats])
         return 0
 
     lax.fori_loop(0, slots, bands, 0)
@@ -503,19 +518,27 @@
 
     def run(c, s):
         brick = bricks[s]
-        fetch(s, c).wait()
+        if c == 0:
+            fetch(s).wait()
 
         def emit(rows, value):
             factors[s, c, rows, :] = value
 
+        line = 2 * (by + 2 * halo)
+
+        def view(x, count):
+            return seen_views[s, pl.ds(pl.multiple_of(x * line, 16), count * line), :]
+
         job(
+            c,
             lambda y, count: blocks[c][pl.ds(brick * by + y, count)],
-            lambda x: seen_views[s, c, x],
+            view,
             background[slot_views[s]],
             dims,
             [m.at[s] for m in mats],
             s1,
             s2,
+            vf,
             emit,
         )
 
@@ -552,12 +575,12 @@
         seen = seen + crossing[k]
     seen = seen.astype(F32)
     f.total(0)
-    update(0, estimate, out, f.final, seen)
+    update(0, bx, by, estimate, out, f.final, seen)
     f.send(1)
     for c in range(2):
         g.finish(c)
     f.total(1)
-    update(1, estimate, out, f.final, seen)
+    update(1, bx, by, estimate, out, f.final, seen)
     for c in range(2):
         f.finish(c)
 
@@ -568,17 +591,18 @@
     halo = taps // 2
     dims = (taps, halo, bx, by, nz)
     slots, px, py = slot_brick.shape[2], bx + 2 * halo, by + 2 * halo
-    est_wire = jnp.swapaxes(estimate.astype(BF16), 1, 2)
-    wire = jnp.concatenate([est_wire[:, :, :HB], est_wire[:, :, bx - HB :]], axis=2)
+    cells = jnp.transpose(estimate, (1, 2, 0, 3)).reshape(bx * by * channels, nz)
+    views = jnp.transpose(view_data[0, 0], (0, 2, 3, 1, 4)).reshape(slots, px * py * channels, nz)
     count = 2 * halo + by * n + ROWS - py
-    return pl.pallas_call(
+    updated = pl.pallas_call(
         functools.partial(kernel, n, nv, dims),
-        out_shape=jax.ShapeDtypeStruct(estimate.shape, F32),
-        in_specs=[VMEM, VMEM, pl.BlockSpec(memory_space=pl.ANY)] + [SMEM] * 5,
+        out_shape=jax.ShapeDtypeStruct(cells.shape, F32),
+        in_specs=[VMEM, pl.BlockSpec(memory_space=pl.ANY)] + [SMEM] * 5,
         out_specs=VMEM,
-        scratch_shapes=[pltpu.VMEM((count, ROWS, nz), BF16)] * 2
-        + [pltpu.VMEM((slots, channels, px, py, nz), BF16), pltpu.SemaphoreType.DMA((slots, channels))]
-        + job_scratch(slots, nz)
+        scratch_shapes=[pltpu.VMEM((channels, by, UP, nz), BF16)]
+        + [pltpu.VMEM((count, ROWS, nz), BF16)] * 2
+        + [pltpu.VMEM((slots, px * py * channels, nz), BF16), pltpu.SemaphoreType.DMA((slots,))]
+        + job_scratch(slots, py, nz)
         + scatter_scratch(n, slots, by, nz)
         + gather_sems(n)
         + scatter_sems(n),
@@ -586,15 +610,15 @@
             collective_id=0, has_side_effects=True, vmem_limit_bytes=60 * 1024 * 1024
         ),
     )(
-        wire,
-        estimate,
-        view_data[0, 0],
-        psf.reshape(-1),
+        cells,
+        views,
+        psf,
         background,
         slot_brick[0, 0],
         slot_view[0, 0],
         intersection[0, 0],
     )
+    return jnp.transpose(updated.reshape(bx, by, channels, nz), (2, 0, 1, 3))
 
 
 def solution(mesh):

time: 101 us -> 80.9 us (0.80)
  Pallas kernels: 87.2 us -> 78.6 us
  local copies, waits for them, and re-layouts: 10.4 us -> 2.08 us
  other arithmetic: 2.36 us -> 0 us
    pallas_call x1, Pallas kernels: 87.2 us -> 78.6 us  [on_device(): pl.pallas_call(functools.partial(kernel, n, nv, dims), out_shape=jax.Shap...]
    unnamed x4 -> x1, local copies, waits for them, and re-layouts: 6.19 us -> 2.08 us
    pallas_call x1 -> x0, local copies, waits for them, and re-layouts: 2.69 us -> none  [on_device(): pl.pallas_call(functools.partial(kernel, n, nv, dims), out_shape=jax.Shap...]
    convert_element_type x1 -> x0, other arithmetic: 1.56 us -> none  [on_device(): est_wire = jnp.swapaxes(estimate.astype(BF16), 1, 2)]
    reshape x1 -> x0, local copies, waits for them, and re-layouts: 1.38 us -> none  [on_device(): psf.reshape(-1)]
where the time goes in v4:
time: 80.9 us; the launch traced here: 80.7 us
  Pallas kernels  78.6 us (97%)
  local copies, waits for them, and re-layouts  2.08 us (3%)
    pallas_call x1, Pallas kernels, on_device(): pl.pallas_call(functools.partial(kernel, n, nv, dims), out_shape=jax.Shap...  78.6 us
    unnamed x1, local copies, waits for them, and re-layouts  2.08 us

profile of v4, /device:TPU:0, one launch (start us, length us, event | category | flops | bytes accessed | tf_op | source)
XLA Modules:
  0.0 80.7 jit_solution(12282258822452433323)
XLA Ops:
  0.0 78.6 %shard_map.73 = f32[1568,128]{1,0:T(8,128)} custom-call(f32[1568,128]{1,0:T(8,128)} %bitcast.16, bf16[3,6728,128]{2,1,0:T(8,128)(2,1)} %bitcast.14, f32[6,3,31]{2,1,0:T(4,128)} %psf.1, f32[6]{0:T(128)} %background.1, s32[3]{0:T(128)} %bitcast.17, s32[3]{0:T(128)} %bitcast.18, s32[6]{0:T(128)} %bitcast.19), custom_call_target="tpu_custom_call" | custom-call | tf_op jit(solution)/shard_map/pallas_call | solution.py:597
  78.6 2.1 %copy.9 = f32[2,28,28,128]{3,0,2,1:T(2,128)} copy(f32[2,28,28,128]{3,0,2,1:T(2,128)} %bitcast.15) | data formatting | bytes 1605632

commit v5 on v4

--- a/solution.py
+++ b/solution.py
@@ -219,41 +219,48 @@
     taps, halo, bx, by, nz = dims
     px, py = bx + 2 * halo, by + 2 * halo
 
-    def pieces(value, low):
-        hi, lo = split(value)
-        return jnp.where(low, lo.astype(F32), hi.astype(F32)).astype(BF16)
-
-    p, col = iota((ROWS, 3 * ROWS), 0), iota((ROWS, 3 * ROWS), 1)
-    low = (col >= ROWS) & (col < 2 * ROWS)
-    r = jnp.where(col >= 2 * ROWS, col - 2 * ROWS, jnp.where(col >= ROWS, col - ROWS, col))
+    def keep(ref, value):
+        ref[...] = jnp.concatenate(split(value), axis=0)
+
+    p, col = iota((ROWS, 2 * ROWS), 0), iota((ROWS, 2 * ROWS), 1)
+    r = jnp.where(col >= ROWS, col - ROWS, col)
     gap = 2 * HB - (bx - HB) + HB
     x = jnp.where(r < 2 * HB, r - HB, r - gap + HB)
     fresh = (r < 2 * HB) | (x >= HB)
     q = x + halo
     valid = fresh & (q >= 0) & (q < px) & (p < px)
-    fx[...] = pieces(band(lambda k: tap(0, k), taps, q - p + halo, valid), low)
-    fy[...] = pieces(band(lambda k: tap(1, k), taps, r - p + halo, (r < py) & (p < py)), low)
-    p, r, low = p[:UP], r[:UP], low[:UP]
-    cx[...] = pieces(band(lambda k: tap(0, k), taps, p - r + 2 * halo, (r < px) & (p < bx)), low)
-    cy[...] = pieces(band(lambda k: tap(1, k), taps, p - r + 2 * halo, (r < py) & (p < by)), low)
+    keep(fx, band(lambda k: tap(0, k), taps, q - p + halo, valid)[:, :ROWS])
+    keep(fy, band(lambda k: tap(1, k), taps, r - p + halo, (r < py) & (p < py)))
+    p, r = p[:UP], r[:UP]
+    keep(cx, band(lambda k: tap(0, k), taps, p - r + 2 * halo, (r < px) & (p < bx)))
+    keep(cy, band(lambda k: tap(1, k), taps, p - r + 2 * halo, (r < py) & (p < by)))
     z, w = iota((nz, nz), 0), iota((nz, nz), 1)
-    hi, lo = split(band(lambda k: tap(2, k), taps, z - w + halo, w < nz))
-    fz[...] = jnp.concatenate([hi, lo], axis=0)
-    hi, lo = split(band(lambda k: tap(2, k), taps, w - z + halo, w < nz))
-    back = jnp.concatenate([hi, lo], axis=1)
-    cz[...] = jnp.concatenate([back, back], axis=0)
-
-
-def stack(a, b):
-    ah, al = split(a)
-    bh, bl = split(b)
-    hi = jnp.concatenate([ah, bh], axis=1)
-    lo = jnp.concatenate([al, bl], axis=1)
-    return jnp.concatenate([hi, hi, lo], axis=0)
+    for ref, offset in ((fz, z - w), (cz, w - z)):
+        both = jnp.concatenate(split(band(lambda k: tap(2, k), taps, offset + halo, w < nz)), axis=1)
+        ref[...] = jnp.concatenate([both, both], axis=0)
 
 
 def dot(a, b):
     return jnp.dot(a, b, preferred_element_type=F32)
+
+
+def along(mat, a, b):
+    both = jnp.concatenate([a, b], axis=1)
+    if both.dtype != BF16:
+        both = jnp.concatenate(split(both), axis=0)
+    out = dot(mat[...], both)
+    half = out.shape[0] // 2
+    return out[:half] + out[half:]
+
+
+def along_last(x, mat):
+    out = dot(jnp.concatenate(split(x), axis=1), mat[...])
+    half = out.shape[1] // 2
+    return out[:, :half] + out[:, half:]
+
+
+def apart(pairs, nz):
+    return jnp.concatenate([v for f in pairs for v in (f[:, :nz], f[:, nz:])], axis=0)
 
 
 def in_groups(count, size, body):
@@ -279,12 +286,11 @@
         ref[pl.ds(pl.multiple_of((line + 1) * pitch, 8), size), :] = value[:, nz:]
 
     def first(y, count):
-        e = block(y, count).reshape(count * ROWS, nz)
-        t = dot(jnp.concatenate([e, e], axis=1), fz[...])
-        lines = [t[j * ROWS : (j + 1) * ROWS] for j in range(count)]
-        done = [dot(fx[...], stack(lines[j], lines[j + 1])) for j in range(0, count, 2)]
-        for j, u in enumerate(done):
-            put(s1, y + 2 * j, PITCH1, ROWS, u)
+        e = block(y, count)
+        u = apart([along(fx, e[j], e[j + 1]) for j in range(0, count, 2)], nz)
+        t = along_last(u, fz)
+        for j in range(count):
+            s1[pl.ds(pl.multiple_of((y + j) * PITCH1, 8), ROWS), :] = t[j * ROWS : (j + 1) * ROWS]
 
     in_groups(ROWS, 16, first)
 
@@ -296,11 +302,11 @@
             x = 2 * (pair + j)
             a = s1[pl.ds(x, ROWS, PITCH1), :]
             b = s1[pl.ds(x + 1, ROWS, PITCH1), :]
-            predicted = dot(fy[...], stack(a, b)) + backdrop
+            predicted = along(fy, a, b) + backdrop
             va = vf[pl.ds(2 * j * line + c, ROWS, 2), :]
             vb = vf[pl.ds((2 * j + 1) * line + c, ROWS, 2), :]
             done.append((va / predicted[:, :nz], vb / predicted[:, nz:]))
-        done = [dot(cy[...], stack(a, b)) for a, b in done]
+        done = [along(cy, a, b) for a, b in done]
         for j, f in enumerate(done):
             put(s2, 2 * (pair + j), PITCH2, UP, f)
 
@@ -312,22 +318,20 @@
             y = 2 * (pair + j)
             a = s2[pl.ds(y, ROWS, PITCH2), :]
             b = s2[pl.ds(y + 1, ROWS, PITCH2), :]
-            done.append(dot(cx[...], stack(a, b)))
-        f = jnp.concatenate([v for f in done for v in (f[:, :nz], f[:, nz:])], axis=0)
-        hi, lo = split(f)
-        out = dot(jnp.concatenate([hi, lo], axis=1), cz[...])
-        emit(pl.ds(pl.multiple_of(pair * 2 * UP, 8), count * 2 * UP), out[:, :nz] + out[:, nz:])
+            done.append(along(cx, a, b))
+        out = along_last(apart(done, nz), cz)
+        emit(pl.ds(pl.multiple_of(pair * 2 * UP, 8), count * 2 * UP), out)
 
     in_groups(by // 2, 14, third)
 
 
 def job_scratch(slots, py, nz):
     return [
-        pltpu.VMEM((slots, ROWS, 3 * ROWS), BF16),
-        pltpu.VMEM((slots, ROWS, 3 * ROWS), BF16),
-        pltpu.VMEM((slots, UP, 3 * ROWS), BF16),
-        pltpu.VMEM((slots, UP, 3 * ROWS), BF16),
-        pltpu.VMEM((slots, 2 * nz, nz), BF16),
+        pltpu.VMEM((slots, 2 * ROWS, ROWS), BF16),
+        pltpu.VMEM((slots, 2 * ROWS, 2 * ROWS), BF16),
+        pltpu.VMEM((slots, 2 * UP, 2 * ROWS), BF16),
+        pltpu.VMEM((slots, 2 * UP, 2 * ROWS), BF16),
+        pltpu.VMEM((slots, 2 * nz, 2 * nz), BF16),
         pltpu.VMEM((slots, 2 * nz, 2 * nz), BF16),
         pltpu.VMEM((ROWS * PITCH1, nz), F32),
         pltpu.VMEM((ROWS * PITCH2, nz), F32),

time: 80.9 us -> 79.5 us (0.983)
  Pallas kernels: 78.6 us -> 77.2 us
    pallas_call x1, Pallas kernels: 78.6 us -> 77.2 us  [on_device(): pl.pallas_call(functools.partial(kernel, n, nv, dims), out_shape=jax.Shap...]
where the time goes in v5:
time: 79.5 us; the launch traced here: 79.3 us
  Pallas kernels  77.2 us (97%)
  local copies, waits for them, and re-layouts  2.08 us (3%)
    pallas_call x1, Pallas kernels, on_device(): pl.pallas_call(functools.partial(kernel, n, nv, dims), out_shape=jax.Shap...  77.2 us
    unnamed x1, local copies, waits for them, and re-layouts  2.08 us

profile of v5, /device:TPU:0, one launch (start us, length us, event | category | flops | bytes accessed | tf_op | source)
XLA Modules:
  0.0 79.3 jit_solution(3768011663795056003)
XLA Ops:
  0.0 77.2 %shard_map.73 = f32[1568,128]{1,0:T(8,128)} custom-call(f32[1568,128]{1,0:T(8,128)} %bitcast.16, bf16[3,6728,128]{2,1,0:T(8,128)(2,1)} %bitcast.14, f32[6,3,31]{2,1,0:T(4,128)} %psf.1, f32[6]{0:T(128)} %background.1, s32[3]{0:T(128)} %bitcast.17, s32[3]{0:T(128)} %bitcast.18, s32[6]{0:T(128)} %bitcast.19), custom_call_target="tpu_custom_call" | custom-call | tf_op jit(solution)/shard_map/pallas_call | solution.py:601
  77.2 2.1 %copy.9 = f32[2,28,28,128]{3,0,2,1:T(2,128)} copy(f32[2,28,28,128]{3,0,2,1:T(2,128)} %bitcast.15) | data formatting | bytes 1605632

commit v6 on v5

--- a/solution.py
+++ b/solution.py
@@ -276,6 +276,15 @@
         body(full * size, count % size)
 
 
+def skewed(items, stages):
+    items, held = list(items), {}
+    for step in range(len(items) + len(stages) - 1):
+        for depth, stage in enumerate(stages):
+            i = step - depth
+            if 0 <= i < len(items):
+                held[i] = stage(items[i], held[i]) if depth else stage(items[i])
+
+
 def job(c, block, view, backdrop, dims, mats, s1, s2, vf, emit):
     fx, fy, cx, cy, fz, cz = mats
     taps, halo, bx, by, nz = dims
@@ -287,40 +296,55 @@
 
     def first(y, count):
         e = block(y, count)
-        u = apart([along(fx, e[j], e[j + 1]) for j in range(0, count, 2)], nz)
-        t = along_last(u, fz)
-        for j in range(count):
-            s1[pl.ds(pl.multiple_of((y + j) * PITCH1, 8), ROWS), :] = t[j * ROWS : (j + 1) * ROWS]
+        part = 4
+
+        def ahead(k):
+            return apart([along(fx, e[j], e[j + 1]) for j in range(k, k + part, 2)], nz)
+
+        def after(k, u):
+            t = along_last(u, fz)
+            for j in range(part):
+                s1[pl.ds(pl.multiple_of((y + k + j) * PITCH1, 8), ROWS), :] = t[j * ROWS : (j + 1) * ROWS]
+
+        skewed(range(0, count, part), [ahead, after])
 
     in_groups(ROWS, 16, first)
 
     def second(pair, count):
-        done = []
         line = 2 * py
         vf[: count * 2 * line, :] = view(2 * pair, 2 * count).astype(F32)
-        for j in range(count):
+
+        def forward(j):
             x = 2 * (pair + j)
-            a = s1[pl.ds(x, ROWS, PITCH1), :]
-            b = s1[pl.ds(x + 1, ROWS, PITCH1), :]
-            predicted = along(fy, a, b) + backdrop
+            return along(fy, s1[pl.ds(x, ROWS, PITCH1), :], s1[pl.ds(x + 1, ROWS, PITCH1), :])
+
+        def ratio(j, blurred):
+            predicted = blurred + backdrop
             va = vf[pl.ds(2 * j * line + c, ROWS, 2), :]
             vb = vf[pl.ds((2 * j + 1) * line + c, ROWS, 2), :]
-            done.append((va / predicted[:, :nz], vb / predicted[:, nz:]))
-        done = [along(cy, a, b) for a, b in done]
-        for j, f in enumerate(done):
-            put(s2, 2 * (pair + j), PITCH2, UP, f)
+            return va / predicted[:, :nz], vb / predicted[:, nz:]
+
+        def back(j, lines):
+            put(s2, 2 * (pair + j), PITCH2, UP, along(cy, *lines))
+
+        skewed(range(count), [forward, ratio, back])
 
     in_groups(px // 2, GROUP, second)
 
     def third(pair, count):
-        done = []
-        for j in range(count):
-            y = 2 * (pair + j)
-            a = s2[pl.ds(y, ROWS, PITCH2), :]
-            b = s2[pl.ds(y + 1, ROWS, PITCH2), :]
-            done.append(along(cx, a, b))
-        out = along_last(apart(done, nz), cz)
-        emit(pl.ds(pl.multiple_of(pair * 2 * UP, 8), count * 2 * UP), out)
+        part = 2
+
+        def ahead(k):
+            lines = []
+            for j in range(k, min(k + part, count)):
+                y = 2 * (pair + j)
+                lines.append(along(cx, s2[pl.ds(y, ROWS, PITCH2), :], s2[pl.ds(y + 1, ROWS, PITCH2), :]))
+            return apart(lines, nz)
+
+        def after(k, f):
+            emit(pl.ds(pl.multiple_of((pair + k) * 2 * UP, 8), f.shape[0]), along_last(f, cz))
+
+        skewed(range(0, count, part), [ahead, after])
 
     in_groups(by // 2, 14, third)
 

time: 79.5 us -> 82.7 us (1.040)
  Pallas kernels: 77.2 us -> 80.5 us
    pallas_call x1, Pallas kernels: 77.2 us -> 80.5 us  [on_device(): pl.pallas_call(functools.partial(kernel, n, nv, dims), out_shape=jax.Shap...]
where the time goes in v6:
time: 82.7 us; the launch traced here: 82.6 us
  Pallas kernels  80.5 us (97%)
  local copies, waits for them, and re-layouts  2.08 us (3%)
    pallas_call x1, Pallas kernels, on_device(): pl.pallas_call(functools.partial(kernel, n, nv, dims), out_shape=jax.Shap...  80.5 us
    unnamed x1, local copies, waits for them, and re-layouts  2.08 us

profile of v6, /device:TPU:0, one launch (start us, length us, event | category | flops | bytes accessed | tf_op | source)
XLA Modules:
  0.0 82.6 jit_solution(8800745986884399269)
XLA Ops:
  0.0 80.5 %shard_map.73 = f32[1568,128]{1,0:T(8,128)} custom-call(f32[1568,128]{1,0:T(8,128)} %bitcast.16, bf16[3,6728,128]{2,1,0:T(8,128)(2,1)} %bitcast.14, f32[6,3,31]{2,1,0:T(4,128)} %psf.1, f32[6]{0:T(128)} %background.1, s32[3]{0:T(128)} %bitcast.17, s32[3]{0:T(128)} %bitcast.18, s32[6]{0:T(128)} %bitcast.19), custom_call_target="tpu_custom_call" | custom-call | tf_op jit(solution)/shard_map/pallas_call | solution.py:625
  80.5 2.1 %copy.9 = f32[2,28,28,128]{3,0,2,1:T(2,128)} copy(f32[2,28,28,128]{3,0,2,1:T(2,128)} %bitcast.15) | data formatting | bytes 1605632

commit v7 on v6

--- a/solution.py
+++ b/solution.py
@@ -15,7 +15,7 @@
 UP = 32
 PITCH1 = 72
 PITCH2 = 40
-GROUP = 8
+GROUP = 10
 VMEM = pl.BlockSpec(memory_space=pltpu.VMEM)
 SMEM = pl.BlockSpec(memory_space=pltpu.SMEM)
 
@@ -276,13 +276,10 @@
         body(full * size, count % size)
 
 
-def skewed(items, stages):
-    items, held = list(items), {}
-    for step in range(len(items) + len(stages) - 1):
-        for depth, stage in enumerate(stages):
-            i = step - depth
-            if 0 <= i < len(items):
-                held[i] = stage(items[i], held[i]) if depth else stage(items[i])
+def staged(items, stages):
+    held = [stages[0](i) for i in items]
+    for stage in stages[1:]:
+        held = [stage(i, h) for i, h in zip(items, held)]
 
 
 def job(c, block, view, backdrop, dims, mats, s1, s2, vf, emit):
@@ -296,7 +293,7 @@
 
     def first(y, count):
         e = block(y, count)
-        part = 4
+        part = count
 
         def ahead(k):
             return apart([along(fx, e[j], e[j + 1]) for j in range(k, k + part, 2)], nz)
@@ -306,7 +303,7 @@
             for j in range(part):
                 s1[pl.ds(pl.multiple_of((y + k + j) * PITCH1, 8), ROWS), :] = t[j * ROWS : (j + 1) * ROWS]
 
-        skewed(range(0, count, part), [ahead, after])
+        staged(range(0, count, part), [ahead, after])
 
     in_groups(ROWS, 16, first)
 
@@ -327,12 +324,12 @@
         def back(j, lines):
             put(s2, 2 * (pair + j), PITCH2, UP, along(cy, *lines))
 
-        skewed(range(count), [forward, ratio, back])
+        staged(range(count), [forward, ratio, back])
 
     in_groups(px // 2, GROUP, second)
 
     def third(pair, count):
-        part = 2
+        part = count
 
         def ahead(k):
             lines = []
@@ -344,7 +341,7 @@
         def after(k, f):
             emit(pl.ds(pl.multiple_of((pair + k) * 2 * UP, 8), f.shape[0]), along_last(f, cz))
 
-        skewed(range(0, count, part), [ahead, after])
+        staged(range(0, count, part), [ahead, after])
 
     in_groups(by // 2, 14, third)
 

time: 82.7 us -> 78.4 us (0.948)
  Pallas kernels: 80.5 us -> 76.2 us
    pallas_call x1, Pallas kernels: 80.5 us -> 76.2 us  [on_device(): pl.pallas_call(functools.partial(kernel, n, nv, dims), out_shape=jax.Shap...]
where the time goes in v7:
time: 78.4 us; the launch traced here: 78.3 us
  Pallas kernels  76.2 us (97%)
  local copies, waits for them, and re-layouts  2.08 us (3%)
    pallas_call x1, Pallas kernels, on_device(): pl.pallas_call(functools.partial(kernel, n, nv, dims), out_shape=jax.Shap...  76.2 us
    unnamed x1, local copies, waits for them, and re-layouts  2.08 us

profile of v7, /device:TPU:0, one launch (start us, length us, event | category | flops | bytes accessed | tf_op | source)
XLA Modules:
  0.0 78.3 jit_solution(6551381699923299190)
XLA Ops:
  0.0 76.2 %shard_map.73 = f32[1568,128]{1,0:T(8,128)} custom-call(f32[1568,128]{1,0:T(8,128)} %bitcast.16, bf16[3,6728,128]{2,1,0:T(8,128)(2,1)} %bitcast.14, f32[6,3,31]{2,1,0:T(4,128)} %psf.1, f32[6]{0:T(128)} %background.1, s32[3]{0:T(128)} %bitcast.17, s32[3]{0:T(128)} %bitcast.18, s32[6]{0:T(128)} %bitcast.19), custom_call_target="tpu_custom_call" | custom-call | tf_op jit(solution)/shard_map/pallas_call | solution.py:622
  76.2 2.1 %copy.9 = f32[2,28,28,128]{3,0,2,1:T(2,128)} copy(f32[2,28,28,128]{3,0,2,1:T(2,128)} %bitcast.15) | data formatting | bytes 1605632
